TPU v7x, 32 devices: a whole 2x2x4 slice. The times are simulated.
32 devices in a mesh: prow: 8 (over z, y), pcol: 4 (over x, core).
Axes of the slice: x: 2, y: 2, z: 4, core: 2. Of those that a mesh axis runs over, the one named last changes fastest.
Arguments:
- right_side: bfloat16 [8, 6, 128, 256], P('prow'), may hold values from -6 to 6
- lower_inverse: bfloat16 [8, 6, 256, 256], P('prow'), as said below
- upper_inverse: bfloat16 [8, 6, 256, 256], P('prow'), as said below
- lower_blocks: bfloat16 [8, 5, 24, 256, 256], P('prow', None, 'pcol'), may hold values from -0.078125 to 0.078125
- lower_sources: int32 [8, 5, 24], P('prow', None, 'pcol'), may hold values from 0 to 39, as said below
- lower_counts: int32 [8, 5, 4], P('prow', None, 'pcol'), may hold values from 1 to 6, as said below
- upper_blocks: bfloat16 [8, 5, 24, 256, 256], P('prow', None, 'pcol'), may hold values from -0.078125 to 0.078125
- upper_sources: int32 [8, 5, 24], P('prow', None, 'pcol'), may hold values from 8 to 47, as said below
- upper_counts: int32 [8, 5, 4], P('prow', None, 'pcol'), may hold values from 1 to 6, as said below
Outputs:
- solution: bfloat16 [8, 6, 128, 256], P('prow')
Inputs may be any that keep to these rules, and one draw needn't show every extreme that they name: `lower_sources`: entry [r, l, c] names supernode v * 8 + p of a level v below l + 1, with p % (4) == c // 6; entries may repeat. `upper_sources`: entry [r, l, c] names supernode v * 8 + p of a level v above l, with p % (4) == c // 6; entries may repeat. `lower_counts`: entry [r, l, g] is how many of the 6 slots of group g are live; the live ones come first. `upper_counts`: entry [r, l, g] is how many of the 6 slots of group g are live; the live ones come first. `lower_inverse`: each block is lower triangular. `upper_inverse`: each block is upper triangular.
All inputs are finite; a program needn't handle non-finite values.
Results may differ from a plain program's by a relative error of at most 0.02.
Values may be sent and summed in bfloat16 or wider, within the bound.
A program may use at most 64 MiB of HBM per device.

v0:
```python
import jax
import jax.numpy as jnp
from jax import lax
from jax.sharding import PartitionSpec as P


def pick_sources(sources, count, store, width, ncol):
    group = store.shape[1]
    flat = store.reshape(store.shape[0] * group, store.shape[2], store.shape[3])
    position = sources // width * group + sources % width // ncol
    picked = flat[position]
    live = jnp.arange(sources.shape[0], dtype=jnp.int32) < count
    return jnp.where(live[:, None, None], picked, jnp.zeros_like(picked))


def contract(picked, blocks):
    return lax.dot_general(
        picked, blocks, (((0, 2), (0, 2)), ((), ())), preferred_element_type=jnp.float32
    )


def apply_inverse(residual, inverse):
    product = lax.dot_general(
        residual, inverse, (((1,), (1,)), ((), ())), preferred_element_type=jnp.float32
    )
    return product.astype(jnp.bfloat16)


def solve_level(right, inverse, blocks, sources, count, store):
    width = lax.axis_size("prow")
    ncol = lax.axis_size("pcol")
    picked = pick_sources(sources, count, store, width, ncol)
    total = lax.psum(contract(picked, blocks), "pcol")
    residual = (right.astype(jnp.float32) - total).astype(jnp.bfloat16)
    return apply_inverse(residual, inverse)


def spread(solved):
    ncol = lax.axis_size("pcol")
    column = lax.axis_index("pcol")
    whole = lax.all_gather(solved[None], "prow", axis=0, tiled=True)
    whole = whole.reshape(whole.shape[0] // ncol, ncol, whole.shape[1], whole.shape[2])
    return lax.dynamic_index_in_dim(whole, column, 1, keepdims=False)


def shards(
    right_side,
    lower_inverse,
    upper_inverse,
    lower_blocks,
    lower_sources,
    lower_counts,
    upper_blocks,
    upper_sources,
    upper_counts,
):
    group = lax.axis_size("prow") // lax.axis_size("pcol")
    levels = right_side.shape[1]
    shape = (levels, group, right_side.shape[2], right_side.shape[3])
    forward_store = jnp.zeros(shape, jnp.bfloat16)
    forward_own = []
    for level in range(levels):
        if level == 0:
            solved = apply_inverse(right_side[0, 0], lower_inverse[0, 0])
        else:
            solved = solve_level(
                right_side[0, level],
                lower_inverse[0, level],
                lower_blocks[0, level - 1],
                lower_sources[0, level - 1],
                lower_counts[0, level - 1, 0],
                forward_store,
            )
        forward_own.append(solved)
        if level + 1 < levels:
            forward_store = forward_store.at[level].set(spread(solved))
    backward_store = jnp.zeros(shape, jnp.bfloat16)
    backward_own = [None] * levels
    for level in range(levels - 1, -1, -1):
        if level == levels - 1:
            solved = apply_inverse(forward_own[level], upper_inverse[0, level])
        else:
            solved = solve_level(
                forward_own[level],
                upper_inverse[0, level],
                upper_blocks[0, level],
                upper_sources[0, level],
                upper_counts[0, level, 0],
                backward_store,
            )
        backward_own[level] = solved
        if level > 0:
            backward_store = backward_store.at[level].set(spread(solved))
    return jnp.stack(backward_own)[None]


def solution(mesh):
    in_specs = (
        P("prow", None, None, None),
        P("prow", None, None, None),
        P("prow", None, None, None),
        P("prow", None, "pcol", None, None),
        P("prow", None, "pcol"),
        P("prow", None, "pcol"),
        P("prow", None, "pcol", None, None),
        P("prow", None, "pcol"),
        P("prow", None, "pcol"),
    )
    out_specs = P("prow", None, None, None)
    return jax.shard_map(shards, mesh=mesh, in_specs=in_specs, out_specs=out_specs, check_vma=False)
```

profile of v0, /device:TPU:0, one launch (start us, length us, event | category | flops | bytes accessed | tf_op | source)
XLA Modules:
  0.0 689.3 jit_solution(3598055458147101026)
XLA Ops:
  6.5 1.2 convolution_convert_fusion.11
  7.8 33.0 %all-gather = bf16[1024,256]{1,0:T(8,128)(2,1)S(1)} all-gather(bf16[128,256]{1,0:T(8,128)(2,1)S(1)} %convolution_convert_fusion.11), channel_id=2, replica_groups=mesh['prow'=8,'pcol'=4] {'prow'}, dimensions={0}, use_global_device_ids=true | all-gather | bytes 589824 | tf_op jit(solution)/shard_map/all_gather | solution.py:41
  40.8 0.9 fusion.107
  41.7 1.5 fusion.124
  43.2 0.6 iota_compare_fusion.7
  43.9 0.6 gather_fusion
  44.5 2.2 convolution_bitcast_fusion.9
  46.8 0.7 fusion.123
  47.6 0.6 iota_compare_fusion.6
  48.2 31.2 %all-reduce.13.cloned.1.call-done = f32[128,256]{1,0:T(8,128)} async-done(((f32[128,256]{1,0:T(8,128)}), f32[128,256]{1,0:T(8,128)}) %all-reduce.13.cloned.1.call-update) | async-done | bytes 131088 | tf_op jit(solution)/shard_map/psum | solution.py:33
  79.4 1.1 convolution_convert_fusion.10
  80.5 31.4 %all-gather.1 = bf16[1024,256]{1,0:T(8,128)(2,1)S(1)} all-gather(bf16[128,256]{1,0:T(8,128)(2,1)S(1)} %convolution_convert_fusion.10), channel_id=3, replica_groups=mesh['prow'=8,'pcol'=4] {'prow'}, dimensions={0}, use_global_device_ids=true | all-gather | bytes 589824 | tf_op jit(solution)/shard_map/all_gather | solution.py:41
  111.9 0.6 gather_fusion.1
  112.4 2.2 convolution_bitcast_fusion.8
  114.7 0.6 iota_compare_fusion.5
  115.4 30.8 %all-reduce.15.cloned.1.call-done = f32[128,256]{1,0:T(8,128)} async-done(((f32[128,256]{1,0:T(8,128)}), f32[128,256]{1,0:T(8,128)}) %all-reduce.15.cloned.1.call-update) | async-done | bytes 131088 | tf_op jit(solution)/shard_map/psum | solution.py:33
  146.2 1.1 convolution_convert_fusion.9
  147.3 31.4 %all-gather.2 = bf16[1024,256]{1,0:T(8,128)(2,1)S(1)} all-gather(bf16[128,256]{1,0:T(8,128)(2,1)S(1)} %convolution_convert_fusion.9), channel_id=4, replica_groups=mesh['prow'=8,'pcol'=4] {'prow'}, dimensions={0}, use_global_device_ids=true | all-gather | bytes 589824 | tf_op jit(solution)/shard_map/all_gather | solution.py:41
  178.7 0.6 gather_fusion.2
  179.2 2.2 convolution_bitcast_fusion.7
  181.5 0.7 iota_compare_fusion.4
  182.2 30.7 %all-reduce.17.cloned.1.call-done = f32[128,256]{1,0:T(8,128)} async-done(((f32[128,256]{1,0:T(8,128)}), f32[128,256]{1,0:T(8,128)}) %all-reduce.17.cloned.1.call-update) | async-done | bytes 131088 | tf_op jit(solution)/shard_map/psum | solution.py:33
  212.9 1.1 convolution_convert_fusion.8
  214.0 31.4 %all-gather.3 = bf16[1024,256]{1,0:T(8,128)(2,1)S(1)} all-gather(bf16[128,256]{1,0:T(8,128)(2,1)S(1)} %convolution_convert_fusion.8), channel_id=5, replica_groups=mesh['prow'=8,'pcol'=4] {'prow'}, dimensions={0}, use_global_device_ids=true | all-gather | bytes 589824 | tf_op jit(solution)/shard_map/all_gather | solution.py:41
  245.4 0.6 gather_fusion.3
  246.0 2.2 convolution_bitcast_fusion.6
  248.3 0.6 iota_compare_fusion.8
  248.9 30.8 %all-reduce.19.cloned.1.call-done = f32[128,256]{1,0:T(8,128)} async-done(((f32[128,256]{1,0:T(8,128)}), f32[128,256]{1,0:T(8,128)}) %all-reduce.19.cloned.1.call-update) | async-done | bytes 131088 | tf_op jit(solution)/shard_map/psum | solution.py:33
  279.7 1.1 convolution_convert_fusion.7
  280.8 31.4 %all-gather.4 = bf16[1024,256]{1,0:T(8,128)(2,1)S(1)} all-gather(bf16[128,256]{1,0:T(8,128)(2,1)S(1)} %convolution_convert_fusion.7), channel_id=6, replica_groups=mesh['prow'=8,'pcol'=4] {'prow'}, dimensions={0}, use_global_device_ids=true | all-gather | bytes 589824 | tf_op jit(solution)/shard_map/all_gather | solution.py:41
  312.2 0.6 gather_fusion.4
  312.8 2.2 convolution_bitcast_fusion.5
  315.0 0.6 iota_compare_fusion.3
  315.6 30.9 %all-reduce.21.cloned.1.call-done = f32[128,256]{1,0:T(8,128)} async-done(((f32[128,256]{1,0:T(8,128)}), f32[128,256]{1,0:T(8,128)}) %all-reduce.21.cloned.1.call-update) | async-done | bytes 131088 | tf_op jit(solution)/shard_map/psum | solution.py:33
  346.5 1.2 convolution_convert_fusion.5
  347.7 31.4 %all-gather.5 = bf16[1024,256]{1,0:T(8,128)(2,1)S(1)} all-gather(bf16[128,256]{1,0:T(8,128)(2,1)S(1)} %convolution_convert_fusion.5), channel_id=7, replica_groups=mesh['prow'=8,'pcol'=4] {'prow'}, dimensions={0}, use_global_device_ids=true | all-gather | bytes 589824 | tf_op jit(solution)/shard_map/all_gather | solution.py:41
  379.2 0.6 gather_fusion.5
  379.7 2.2 convolution_bitcast_fusion.4
  382.0 0.7 iota_compare_fusion.2
  382.7 30.7 %all-reduce.23.cloned.1.call-done = f32[128,256]{1,0:T(8,128)} async-done(((f32[128,256]{1,0:T(8,128)}), f32[128,256]{1,0:T(8,128)}) %all-reduce.23.cloned.1.call-update) | async-done | bytes 131088 | tf_op jit(solution)/shard_map/psum | solution.py:33
  413.4 1.1 convolution_convert_fusion.4
  414.5 31.4 %all-gather.6 = bf16[1024,256]{1,0:T(8,128)(2,1)S(1)} all-gather(bf16[128,256]{1,0:T(8,128)(2,1)S(1)} %convolution_convert_fusion.4), channel_id=8, replica_groups=mesh['prow'=8,'pcol'=4] {'prow'}, dimensions={0}, use_global_device_ids=true | all-gather | bytes 589824 | tf_op jit(solution)/shard_map/all_gather | solution.py:41
  445.9 0.6 gather_fusion.6
  446.5 2.2 convolution_bitcast_fusion.3
  448.8 0.7 iota_compare_fusion.1
  449.5 30.8 %all-reduce.25.cloned.1.call-done = f32[128,256]{1,0:T(8,128)} async-done(((f32[128,256]{1,0:T(8,128)}), f32[128,256]{1,0:T(8,128)}) %all-reduce.25.cloned.1.call-update) | async-done | bytes 131088 | tf_op jit(solution)/shard_map/psum | solution.py:33
  480.2 1.1 convolution_convert_fusion.3
  481.3 31.4 %all-gather.7 = bf16[1024,256]{1,0:T(8,128)(2,1)S(1)} all-gather(bf16[128,256]{1,0:T(8,128)(2,1)S(1)} %convolution_convert_fusion.3), channel_id=9, replica_groups=mesh['prow'=8,'pcol'=4] {'prow'}, dimensions={0}, use_global_device_ids=true | all-gather | bytes 589824 | tf_op jit(solution)/shard_map/all_gather | solution.py:41
  512.7 0.6 gather_fusion.7
  513.3 2.2 convolution_bitcast_fusion.2
  516.1 30.9 %all-reduce.27.cloned.1.call-done = f32[128,256]{1,0:T(8,128)} async-done(((f32[128,256]{1,0:T(8,128)}), f32[128,256]{1,0:T(8,128)}) %all-reduce.27.cloned.1.call-update) | async-done | bytes 131088 | tf_op jit(solution)/shard_map/psum | solution.py:33
  547.0 1.1 convolution_convert_fusion.2
  548.1 31.4 %all-gather.8 = bf16[1024,256]{1,0:T(8,128)(2,1)S(1)} all-gather(bf16[128,256]{1,0:T(8,128)(2,1)S(1)} %convolution_convert_fusion.2), channel_id=10, replica_groups=mesh['prow'=8,'pcol'=4] {'prow'}, dimensions={0}, use_global_device_ids=true | all-gather | bytes 589824 | tf_op jit(solution)/shard_map/all_gather | solution.py:41
  579.5 0.6 gather_fusion.8
  580.0 2.2 convolution_bitcast_fusion.1
  582.3 0.6 iota_compare_fusion.9
  583.0 30.8 %all-reduce.29.cloned.1.call-done = f32[128,256]{1,0:T(8,128)} async-done(((f32[128,256]{1,0:T(8,128)}), f32[128,256]{1,0:T(8,128)}) %all-reduce.29.cloned.1.call-update) | async-done | bytes 131088 | tf_op jit(solution)/shard_map/psum | solution.py:33
  613.7 1.1 convolution_convert_fusion.1
  614.8 31.4 %all-gather.9 = bf16[1024,256]{1,0:T(8,128)(2,1)S(1)} all-gather(bf16[128,256]{1,0:T(8,128)(2,1)S(1)} %convolution_convert_fusion.1), channel_id=11, replica_groups=mesh['prow'=8,'pcol'=4] {'prow'}, dimensions={0}, use_global_device_ids=true | all-gather | bytes 589824 | tf_op jit(solution)/shard_map/all_gather | solution.py:41
  646.2 0.6 gather_fusion.9
  646.8 2.2 convolution_bitcast_fusion
  649.0 31.5 %all-reduce.31.cloned.1.call-done = f32[128,256]{1,0:T(8,128)} async-done(((f32[128,256]{1,0:T(8,128)}), f32[128,256]{1,0:T(8,128)}) %all-reduce.31.cloned.1.call-update) | async-done | bytes 131088 | tf_op jit(solution)/shard_map/psum | solution.py:33
  680.5 1.1 fusion.1
  681.7 0.7 copy-done.4
  (57 shorter events, 1.4 us)
Async XLA Ops:
  6.5 72.8 %copy-start.2 = (bf16[1,6,128,256]{3,2,1,0:T(8,128)(2,1)S(1)}, bf16[1,6,128,256]{3,2,1,0:T(8,128)(2,1)}, u32[]{:S(2)}) copy-start(bf16[1,6,128,256]{3,2,1,0:T(8,128)(2,1)} %param.29) | copy-start | bytes 1179652
  6.5 72.8 %copy-start.1 = (bf16[1,6,256,256]{3,2,1,0:T(8,128)(2,1)S(1)}, bf16[1,6,256,256]{3,2,1,0:T(8,128)(2,1)}, u32[]{:S(2)}) copy-start(bf16[1,6,256,256]{3,2,1,0:T(8,128)(2,1)} %param.30) | copy-start | bytes 2359300
  6.5 40.3 %copy-start.3 = (s32[1,5,1]{1,2,0:T(1,128)S(1)}, s32[1,5,1]{1,2,0:T(1,128)}, u32[]{:S(2)}) copy-start(s32[1,5,1]{1,2,0:T(1,128)} %param.37) | copy-start | bytes 64
  6.5 72.8 %all-reduce.13.cloned.1.call-start = ((), (), s32[]{:S(2)}) async-start(), calls=%async_computation | async-start | bytes 262144 | tf_op jit(solution)/shard_map/psum | solution.py:33
  46.7 99.5 %all-reduce.15.cloned.1.call-start = ((), (), s32[]{:S(2)}) async-start(), calls=%async_computation.1 | async-start | bytes 262144 | tf_op jit(solution)/shard_map/psum | solution.py:33
  114.7 98.3 %all-reduce.17.cloned.1.call-start = ((), (), s32[]{:S(2)}) async-start(), calls=%async_computation.2 | async-start | bytes 262144 | tf_op jit(solution)/shard_map/psum | solution.py:33
  181.5 165.0 %copy-start = (bf16[1,6,256,256]{3,2,1,0:T(8,128)(2,1)S(1)}, bf16[1,6,256,256]{3,2,1,0:T(8,128)(2,1)}, u32[]{:S(2)}) copy-start(bf16[1,6,256,256]{3,2,1,0:T(8,128)(2,1)} %param.31) | copy-start | bytes 2359300
  181.5 98.2 %all-reduce.19.cloned.1.call-start = ((), (), s32[]{:S(2)}) async-start(), calls=%async_computation.3 | async-start | bytes 262144 | tf_op jit(solution)/shard_map/psum | solution.py:33
  248.2 98.3 %all-reduce.21.cloned.1.call-start = ((), (), s32[]{:S(2)}) async-start(), calls=%async_computation.4 | async-start | bytes 262144 | tf_op jit(solution)/shard_map/psum | solution.py:33
  315.0 98.4 %all-reduce.23.cloned.1.call-start = ((), (), s32[]{:S(2)}) async-start(), calls=%async_computation.5 | async-start | bytes 262144 | tf_op jit(solution)/shard_map/psum | solution.py:33
  382.0 98.3 %all-reduce.25.cloned.1.call-start = ((), (), s32[]{:S(2)}) async-start(), calls=%async_computation.6 | async-start | bytes 262144 | tf_op jit(solution)/shard_map/psum | solution.py:33
  448.7 98.3 %all-reduce.27.cloned.1.call-start = ((), (), s32[]{:S(2)}) async-start(), calls=%async_computation.7 | async-start | bytes 262144 | tf_op jit(solution)/shard_map/psum | solution.py:33
  515.5 98.2 %all-reduce.29.cloned.1.call-start = ((), (), s32[]{:S(2)}) async-start(), calls=%async_computation.8 | async-start | bytes 262144 | tf_op jit(solution)/shard_map/psum | solution.py:33
  582.3 98.2 %all-reduce.31.cloned.1.call-start = ((), (), s32[]{:S(2)}) async-start(), calls=%async_computation.9 | async-start | bytes 262144 | tf_op jit(solution)/shard_map/psum | solution.py:33
  681.7 0.7 copy-start.4
Sparse Core Ops, SparseCore 0:
  46.8 32.5 all-reduce.12
  114.8 31.3 all-reduce.14
  181.6 31.3 all-reduce.16
  248.3 31.3 all-reduce.18
  315.1 31.3 all-reduce.20
  382.1 31.3 all-reduce.22
  448.8 31.3 all-reduce.24
  515.6 31.3 all-reduce.26
  582.4 31.2 all-reduce.28
  649.1 31.3 all-reduce.30
where the time goes:
time: 690 us; the launch traced here: 689 us
  blocking collectives  315 us (46%)
  waiting for transfers between devices  309 us (45%)
  matrix products  34.2 us (5%)
  between operations  14 us (2%)
  local copies, waits for them, and re-layouts  8.9 us (1%)
  other arithmetic  7.28 us (1%)
    all_gather x10, blocking collectives, spread(): whole = lax.all_gather(solved[None], 'prow', axis=0, tiled=True)  315 us
    psum x10, waiting for transfers between devices, solve_level(): total = lax.psum(contract(picked, blocks), 'pcol')  309 us
    dot_general x10, matrix products, contract(): lax.dot_general(picked, blocks, (((0, 2), (0, 2)), ((), ())), preferred_e...  21.9 us
  transfers between devices with their start and end apart: 10, of which 10 were waited for; matrix products, arithmetic and copies ran while one was open for 1% of the time, Pallas kernels for 0%

commit v1 on v0

v1 whole, which is shorter than its diff:
```python
import functools

import jax
import jax.numpy as jnp
from jax import lax
from jax.experimental import pallas as pl
from jax.experimental.pallas import tpu as pltpu
from jax.sharding import PartitionSpec as P

MESH = pl.DeviceIdType.MESH
NT = (((1,), (1,)), ((), ()))


def product(rows, matrix):
    return lax.dot_general(rows, matrix, NT, preferred_element_type=jnp.float32)


def kernel(
    width, ncol,
    right_hbm, linv_hbm, uinv_hbm, lblk_hbm, lsrc, lcnt, ublk_hbm, usrc, ucnt,
    out_hbm,
    right, linv, uinv, lblk, ublk, fown, bown, part, term, red, land, fstore, bstore,
    right_sem, linv_sem, uinv_sem, lblk_sem, ublk_sem,
    part_send, part_recv, cast_send, cast_recv, out_send, out_recv,
):
    levels, piece, sn = right.shape
    slots = lblk.shape[1]
    group = width // ncol
    nrhs = piece * ncol
    last = levels - 1
    p = lax.axis_index("prow")
    q = lax.axis_index("pcol")
    column = lax.rem(p, ncol)
    mine = pl.ds(pl.multiple_of(q * piece, piece), piece)

    def load_lower(l):
        return pltpu.make_async_copy(lblk_hbm.at[0, l], lblk.at[l], lblk_sem.at[l])

    def load_upper(l):
        return pltpu.make_async_copy(ublk_hbm.at[0, l], ublk.at[l], ublk_sem.at[l])

    def load_linv(l):
        return pltpu.make_async_copy(linv_hbm.at[0, l], linv.at[l], linv_sem.at[l])

    def load_uinv(l):
        return pltpu.make_async_copy(uinv_hbm.at[0, l], uinv.at[l], uinv_sem.at[l])

    load_right = pltpu.make_async_copy(right_hbm.at[0, :, mine], right, right_sem)
    load_linv(0).start()
    load_right.start()
    for l in range(last):
        load_lower(l).start()
        load_linv(l + 1).start()
    load_uinv(last).start()
    for l in range(last - 1, -1, -1):
        load_upper(l).start()
        load_uinv(l).start()

    barrier = pltpu.get_barrier_semaphore()
    for o in range(1, ncol):
        pl.semaphore_signal(barrier, inc=1, device_id=(p, lax.rem(q + o, ncol)), device_id_type=MESH)
    for g in range(group):
        row = q + g * ncol

        @pl.when(row != p)
        def _():
            for c in range(ncol):
                pl.semaphore_signal(barrier, inc=1, device_id=(row, c), device_id_type=MESH)

    fstore[levels * group] = jnp.zeros((nrhs, sn), jnp.bfloat16)
    bstore[levels * group] = jnp.zeros((nrhs, sn), jnp.bfloat16)
    pl.semaphore_wait(barrier, width + ncol - 2)

    slot_rows = pl.ds(pl.multiple_of(p // ncol * nrhs + q * piece, piece), piece)

    def cast_copy(own, l, step, row):
        return pltpu.make_async_remote_copy(
            src_ref=own.at[l], dst_ref=land.at[step, slot_rows],
            send_sem=cast_send.at[step], recv_sem=cast_recv.at[step],
            device_id=(row, column), device_id_type=MESH,
        )

    def cast(own, l, step):
        for j in range(1, width):
            cast_copy(own, l, step, lax.rem(p + j, width)).start()

        @pl.when(q != column)
        def _():
            cast_copy(own, l, step, p).start()

        @pl.when(q == column)
        def _():
            pltpu.make_async_copy(own.at[l], land.at[step, slot_rows], cast_recv.at[step]).start()

    def receive(store, l, step):
        whole = land.at[step]
        pltpu.make_async_copy(whole, whole, cast_recv.at[step]).wait()
        for g in range(group):
            store[l * group + g] = land[step, pl.ds(g * nrhs, nrhs)]

    def solve(step, at, row, right_ref, inverse, blocks, sources, counts, store, own):
        count = counts[0, at, 0]
        total = None
        for c in range(slots):
            source = sources[0, at, c]
            place = lax.div(source, width) * group + lax.div(lax.rem(source, width), ncol)
            place = jnp.where(c < count, place, levels * group)
            now = product(store[place], blocks[at, c])
            total = now if total is None else total + now
        term[...] = total
        part[step] = total.astype(jnp.bfloat16)
        for o in range(1, ncol):
            peer = lax.rem(q + o, ncol)
            pltpu.make_async_remote_copy(
                src_ref=part.at[step, pl.ds(pl.multiple_of(peer * piece, piece), piece)],
                dst_ref=red.at[step, o - 1],
                send_sem=part_send.at[step], recv_sem=part_recv.at[step],
                device_id=(p, peer), device_id_type=MESH,
            ).start()
        update = term[mine]
        arrived = red.at[step]
        pltpu.make_async_copy(arrived, arrived, part_recv.at[step]).wait()
        for o in range(ncol - 1):
            update = update + red[step, o].astype(jnp.float32)
        residual = (right_ref[row].astype(jnp.float32) - update).astype(jnp.bfloat16)
        own[row] = product(residual, inverse[row]).astype(jnp.bfloat16)

    def hand_out(l):
        place = out_hbm.at[0, l, mine]
        for o in range(1, ncol):
            pltpu.make_async_remote_copy(
                src_ref=bown.at[l], dst_ref=place,
                send_sem=out_send.at[l], recv_sem=out_recv,
                device_id=(p, lax.rem(q + o, ncol)), device_id_type=MESH,
            ).start()
        pltpu.make_async_copy(bown.at[l], place, out_recv).start()

    load_linv(0).wait()
    load_right.wait()
    fown[0] = product(right[0], linv[0]).astype(jnp.bfloat16)
    cast(fown, 0, 0)

    def forward(l, _):
        load_lower(l - 1).wait()
        load_linv(l).wait()
        receive(fstore, l - 1, l - 1)
        solve(l - 1, l - 1, l, right, linv, lblk, lsrc, lcnt, fstore, fown)

        @pl.when(l < last)
        def _():
            cast(fown, l, l)

        return 0

    lax.fori_loop(1, levels, forward, 0)

    load_uinv(last).wait()
    bown[last] = product(fown[last], uinv[last]).astype(jnp.bfloat16)
    cast(bown, last, last)
    hand_out(last)

    def backward(i, _):
        l = last - 1 - i
        step = last + i
        load_upper(l).wait()
        load_uinv(l).wait()
        receive(bstore, l + 1, step)
        solve(step, l, l, fown, uinv, ublk, usrc, ucnt, bstore, bown)

        @pl.when(l > 0)
        def _():
            cast(bown, l, step + 1)

        hand_out(l)
        return 0

    lax.fori_loop(0, last, backward, 0)

    def drain(step, _):
        sent = red.at[step]
        pltpu.make_async_copy(sent, sent, part_send.at[step]).wait()
        sent = land.at[step, pl.ds(0, (width - 1) * piece)]
        pltpu.make_async_copy(sent, sent, cast_send.at[step]).wait()

        @pl.when(q != column)
        def _():
            one = land.at[step, pl.ds(0, piece)]
            pltpu.make_async_copy(one, one, cast_send.at[step]).wait()

        return 0

    lax.fori_loop(0, 2 * last, drain, 0)
    for l in range(levels):
        sent = red.at[0]
        pltpu.make_async_copy(sent, sent, out_send.at[l]).wait()
    pltpu.make_async_copy(out_hbm.at[0], out_hbm.at[0], out_recv).wait()


def shards(right_side, lower_inverse, upper_inverse, lower_blocks, lower_sources, lower_counts,
           upper_blocks, upper_sources, upper_counts):
    width = lax.axis_size("prow")
    ncol = lax.axis_size("pcol")
    group = width // ncol
    _, levels, nrhs, sn = right_side.shape
    slots = lower_blocks.shape[2]
    piece = nrhs // ncol
    steps = 2 * (levels - 1)
    bf16 = jnp.bfloat16
    anywhere = pl.BlockSpec(memory_space=pl.ANY)
    scalars = pl.BlockSpec(memory_space=pltpu.SMEM)
    dma = pltpu.SemaphoreType.DMA
    return pl.pallas_call(
        functools.partial(kernel, width, ncol),
        out_shape=jax.ShapeDtypeStruct(right_side.shape, bf16),
        in_specs=[anywhere, anywhere, anywhere, anywhere, scalars, scalars, anywhere, scalars, scalars],
        out_specs=anywhere,
        scratch_shapes=[
            pltpu.VMEM((levels, piece, sn), bf16),
            pltpu.VMEM((levels, sn, sn), bf16),
            pltpu.VMEM((levels, sn, sn), bf16),
            pltpu.VMEM((levels - 1, slots, sn, sn), bf16),
            pltpu.VMEM((levels - 1, slots, sn, sn), bf16),
            pltpu.VMEM((levels, piece, sn), bf16),
            pltpu.VMEM((levels, piece, sn), bf16),
            pltpu.VMEM((steps, nrhs, sn), bf16),
            pltpu.VMEM((nrhs, sn), jnp.float32),
            pltpu.VMEM((steps, ncol - 1, piece, sn), bf16),
            pltpu.VMEM((steps, group * nrhs, sn), bf16),
            pltpu.VMEM((levels * group + 1, nrhs, sn), bf16),
            pltpu.VMEM((levels * group + 1, nrhs, sn), bf16),
            dma, dma((levels,)), dma((levels,)), dma((levels - 1,)), dma((levels - 1,)),
            dma((steps,)), dma((steps,)), dma((steps,)), dma((steps,)), dma((levels,)), dma,
        ],
        compiler_params=pltpu.CompilerParams(
            collective_id=0, has_side_effects=True, vmem_limit_bytes=60 * 1024 * 1024
        ),
        cost_estimate=pl.CostEstimate(flops=1200000000, bytes_accessed=10000000, transcendentals=0),
    )(right_side, lower_inverse, upper_inverse, lower_blocks, lower_sources, lower_counts,
      upper_blocks, upper_sources, upper_counts)


def solution(mesh):
    in_specs = (
        P("prow", None, None, None),
        P("prow", None, None, None),
        P("prow", None, None, None),
        P("prow", None, "pcol", None, None),
        P("prow", None, "pcol"),
        P("prow", None, "pcol"),
        P("prow", None, "pcol", None, None),
        P("prow", None, "pcol"),
        P("prow", None, "pcol"),
    )
    out_specs = P("prow", None, None, None)
    return jax.shard_map(shards, mesh=mesh, in_specs=in_specs, out_specs=out_specs, check_vma=False)
```

time: 690 us -> 103 us (0.15)
  blocking collectives: 315 us -> 0 us
  waiting for transfers between devices: 309 us -> 0 us
  Pallas kernels: 0 us -> 95.4 us
  matrix products: 34.2 us -> 0 us
  between operations: 14 us -> 0.01 us
  other arithmetic: 7.28 us -> 0 us
    all_gather x10 -> x0, blocking collectives: 315 us -> none  [spread(): whole = lax.all_gather(solved[None], 'prow', axis=0, tiled=True)]
    psum x10 -> x0, waiting for transfers between devices: 309 us -> none  [solve_level(): total = lax.psum(contract(picked, blocks), 'pcol')]
    pallas_call x0 -> x1, Pallas kernels: none -> 95.4 us  [shards(): pl.pallas_call(functools.partial(kernel, width, ncol), out_shape=jax.Shap...]
    dot_general x21 -> x0, matrix products: 34.2 us -> none  [the longest x10 21.9 us: contract(): lax.dot_general(picked, blocks, (((0, 2), (0, 2)), ((), ())), preferred_e...]
  transfers between devices with their start and end apart: 10 -> 0, of which waited for: 10 -> 0; matrix products, arithmetic and copies ran while one was open for 1% -> 0% of each run, Pallas kernels for 0% -> 0%
where the time goes in v1:
time: 103 us; the launch traced here: 102 us
  Pallas kernels  95.4 us (93%)
  local copies, waits for them, and re-layouts  6.96 us (7%)
    pallas_call x1, Pallas kernels, shards(): pl.pallas_call(functools.partial(kernel, width, ncol), out_shape=jax.Shap...  95.4 us
    unnamed x5, local copies, waits for them, and re-layouts  6.96 us

profile of v1, /device:TPU:0, one launch (start us, length us, event | category | flops | bytes accessed | tf_op | source)
XLA Modules:
  0.0 102.4 jit_solution(13136991277931855571)
XLA Ops:
  0.0 1.3 %copy.10.lsrc = s32[1,5,6]{2,1,0:T(8,128)} copy(s32[1,5,6]{2,0,1:T(1,128)} %param.13) | data formatting | bytes 240 | tf_op args[4]
  1.3 1.3 %copy.11.lcnt = s32[1,5,1]{2,1,0:T(8,128)} copy(s32[1,5,1]{1,2,0:T(1,128)} %param.14) | data formatting | bytes 40 | tf_op args[5]
  2.6 1.3 %copy.12.usrc = s32[1,5,6]{2,1,0:T(8,128)} copy(s32[1,5,6]{2,0,1:T(1,128)} %param.16) | data formatting | bytes 240 | tf_op args[7]
  3.9 1.3 %copy.13.ucnt = s32[1,5,1]{2,1,0:T(8,128)} copy(s32[1,5,1]{1,2,0:T(1,128)} %param.17) | data formatting | bytes 40 | tf_op args[8]
  5.2 95.4 %shard_map.91 = bf16[1,6,128,256]{3,2,1,0:T(8,128)(2,1)} custom-call(bf16[1,6,128,256]{3,2,1,0:T(8,128)(2,1)} %right_hbm.1, bf16[1,6,256,256]{3,2,1,0:T(8,128)(2,1)} %linv_hbm.1, bf16[1,6,256,256]{3,2,1,0:T(8,128)(2,1)} %uinv_hbm.1, bf16[1,5,6,256,256]{4,3,2,1,0:T(8,128)(2,1)} %lblk_hbm.1, s32[1,5,6]{2,1,0:T(8,128)} %copy.10.lsrc, s32[1,5,1]{2,1,0:T(8,128)} %copy.11.lcnt, ...), custom_call_target="tpu_custom_call" | custom-call | flops 1200000000 | bytes 10000000 | tf_op jit(solution)/shard_map/pallas_call | solution.py:212
  100.6 1.8 %copy.15 = bf16[1,6,128,256]{3,2,1,0:T(8,128)(2,1)} copy(bf16[1,6,128,256]{3,2,1,0:T(8,128)(2,1)} %shard_map.91) | data formatting | bytes 786432

commit v2 on v1

v2 whole, which is shorter than its diff:
```python
import functools

import jax
import jax.numpy as jnp
from jax import lax
from jax.experimental import pallas as pl
from jax.experimental.pallas import tpu as pltpu
from jax.sharding import PartitionSpec as P

MESH = pl.DeviceIdType.MESH
NT = (((1,), (1,)), ((), ()))


def product(rows, matrix):
    return lax.dot_general(rows, matrix, NT, preferred_element_type=jnp.float32)


def kernel(
    width, ncol, chains,
    right_hbm, linv_hbm, uinv_hbm, lblk_hbm, lsrc, lcnt, ublk_hbm, usrc, ucnt,
    out_hbm,
    right, linv, uinv, lblk, ublk, fown, bown, part, term, red, land, fstore, bstore,
    right_sem, linv_sem, uinv_sem, lblk_sem, ublk_sem,
    part_send, part_recv, cast_send, cast_recv, out_send, out_recv,
):
    levels, piece, sn = right.shape
    slots = lblk.shape[1]
    group = width // ncol
    nrhs = piece * ncol
    rows = piece // chains
    span = nrhs // chains
    last = levels - 1
    p = lax.axis_index("prow")
    q = lax.axis_index("pcol")
    column = lax.rem(p, ncol)
    mine = pl.ds(pl.multiple_of(q * piece, piece), piece)

    def load_lower(l):
        return pltpu.make_async_copy(lblk_hbm.at[0, l], lblk.at[l], lblk_sem.at[l])

    def load_upper(l):
        return pltpu.make_async_copy(ublk_hbm.at[0, l], ublk.at[l], ublk_sem.at[l])

    def load_linv(l):
        return pltpu.make_async_copy(linv_hbm.at[0, l], linv.at[l], linv_sem.at[l])

    def load_uinv(l):
        return pltpu.make_async_copy(uinv_hbm.at[0, l], uinv.at[l], uinv_sem.at[l])

    load_right = pltpu.make_async_copy(right_hbm.at[0, :, mine], right, right_sem)
    load_linv(0).start()
    load_right.start()
    for l in range(last):
        load_lower(l).start()
        load_linv(l + 1).start()
    load_uinv(last).start()
    for l in range(last - 1, -1, -1):
        load_upper(l).start()
        load_uinv(l).start()

    barrier = pltpu.get_barrier_semaphore()
    for o in range(1, ncol):
        pl.semaphore_signal(barrier, inc=1, device_id=(p, lax.rem(q + o, ncol)), device_id_type=MESH)
    for g in range(group):
        row = q + g * ncol

        @pl.when(row != p)
        def _():
            for c in range(ncol):
                pl.semaphore_signal(barrier, inc=1, device_id=(row, c), device_id_type=MESH)

    for k in range(chains):
        fstore[k, levels * group] = jnp.zeros((span, sn), jnp.bfloat16)
        bstore[k, levels * group] = jnp.zeros((span, sn), jnp.bfloat16)
    pl.semaphore_wait(barrier, width + ncol - 2)

    slot_rows = pl.ds(pl.multiple_of(p // ncol * span + q * rows, rows), rows)

    def cast_copy(own, l, step, k, row):
        return pltpu.make_async_remote_copy(
            src_ref=own.at[l, pl.ds(k * rows, rows)], dst_ref=land.at[step, k, slot_rows],
            send_sem=cast_send.at[step], recv_sem=cast_recv.at[step, k],
            device_id=(row, column), device_id_type=MESH,
        )

    def cast(own, l, step, k):
        for j in range(1, width):
            cast_copy(own, l, step, k, lax.rem(p + j, width)).start()

        @pl.when(q != column)
        def _():
            cast_copy(own, l, step, k, p).start()

        @pl.when(q == column)
        def _():
            pltpu.make_async_copy(
                own.at[l, pl.ds(k * rows, rows)], land.at[step, k, slot_rows], cast_recv.at[step, k]
            ).start()

    def receive(store, l, step, k):
        whole = land.at[step, k]
        pltpu.make_async_copy(whole, whole, cast_recv.at[step, k]).wait()
        for g in range(group):
            store[k, l * group + g] = land[step, k, pl.ds(g * span, span)]

    def contract(step, at, k, blocks, sources, counts, store):
        count = counts[0, 0, at]
        total = None
        for c in range(slots):
            source = sources[at, 0, c]
            place = lax.div(source, width) * group + lax.div(lax.rem(source, width), ncol)
            place = jnp.where(c < count, place, levels * group)
            now = product(store[k, place], blocks[at, c])
            total = now if total is None else total + now
        part[step, k] = total.astype(jnp.bfloat16)
        for o in range(1, ncol):
            peer = lax.rem(q + o, ncol)
            pltpu.make_async_remote_copy(
                src_ref=part.at[step, k, pl.ds(pl.multiple_of(peer * rows, rows), rows)],
                dst_ref=red.at[step, k, o - 1],
                send_sem=part_send.at[step], recv_sem=part_recv.at[step, k],
                device_id=(p, peer), device_id_type=MESH,
            ).start()
        term[k] = total

    def finish(step, row, k, right_ref, inverse, own):
        update = term[k, pl.ds(pl.multiple_of(q * rows, rows), rows)]
        arrived = red.at[step, k]
        pltpu.make_async_copy(arrived, arrived, part_recv.at[step, k]).wait()
        for o in range(ncol - 1):
            update = update + red[step, k, o].astype(jnp.float32)
        here = pl.ds(k * rows, rows)
        residual = (right_ref[row, here].astype(jnp.float32) - update).astype(jnp.bfloat16)
        own[row, here] = product(residual, inverse[row]).astype(jnp.bfloat16)

    def hand_out(l):
        place = out_hbm.at[0, l, mine]
        for o in range(1, ncol):
            pltpu.make_async_remote_copy(
                src_ref=bown.at[l], dst_ref=place,
                send_sem=out_send.at[l], recv_sem=out_recv,
                device_id=(p, lax.rem(q + o, ncol)), device_id_type=MESH,
            ).start()
        pltpu.make_async_copy(bown.at[l], place, out_recv).start()

    load_linv(0).wait()
    load_right.wait()
    fown[0] = product(right[0], linv[0]).astype(jnp.bfloat16)
    for k in range(chains):
        cast(fown, 0, 0, k)

    def forward(l, _):
        load_lower(l - 1).wait()
        load_linv(l).wait()
        for k in range(chains):
            receive(fstore, l - 1, l - 1, k)
            contract(l - 1, l - 1, k, lblk, lsrc, lcnt, fstore)
        for k in range(chains):
            finish(l - 1, l, k, right, linv, fown)

            @pl.when(l < last)
            def _():
                cast(fown, l, l, k)

        return 0

    lax.fori_loop(1, levels, forward, 0)

    load_uinv(last).wait()
    bown[last] = product(fown[last], uinv[last]).astype(jnp.bfloat16)
    for k in range(chains):
        cast(bown, last, last, k)
    hand_out(last)

    def backward(i, _):
        l = last - 1 - i
        step = last + i
        load_upper(l).wait()
        load_uinv(l).wait()
        for k in range(chains):
            receive(bstore, l + 1, step, k)
            contract(step, l, k, ublk, usrc, ucnt, bstore)
        for k in range(chains):
            finish(step, l, k, fown, uinv, bown)

            @pl.when(l > 0)
            def _():
                cast(bown, l, step + 1, k)

        hand_out(l)
        return 0

    lax.fori_loop(0, last, backward, 0)

    def drain(step, _):
        sent = red.at[step]
        pltpu.make_async_copy(sent, sent, part_send.at[step]).wait()
        for k in range(chains):
            sent = land.at[step, k, pl.ds(0, (width - 1) * rows)]
            pltpu.make_async_copy(sent, sent, cast_send.at[step]).wait()

        @pl.when(q != column)
        def _():
            one = land.at[step, 0, pl.ds(0, piece)]
            pltpu.make_async_copy(one, one, cast_send.at[step]).wait()

        return 0

    lax.fori_loop(0, 2 * last, drain, 0)
    for l in range(levels):
        sent = red.at[0]
        pltpu.make_async_copy(sent, sent, out_send.at[l]).wait()
    pltpu.make_async_copy(out_hbm.at[0], out_hbm.at[0], out_recv).wait()


def shards(right_side, lower_inverse, upper_inverse, lower_blocks, lower_sources, lower_counts,
           upper_blocks, upper_sources, upper_counts):
    width = lax.axis_size("prow")
    ncol = lax.axis_size("pcol")
    group = width // ncol
    _, levels, nrhs, sn = right_side.shape
    slots = lower_blocks.shape[2]
    piece = nrhs // ncol
    chains = 2 if piece % 32 == 0 else 1
    steps = 2 * (levels - 1)
    bf16 = jnp.bfloat16
    anywhere = pl.BlockSpec(memory_space=pl.ANY)
    scalars = pl.BlockSpec(memory_space=pltpu.SMEM)
    dma = pltpu.SemaphoreType.DMA
    return pl.pallas_call(
        functools.partial(kernel, width, ncol, chains),
        out_shape=jax.ShapeDtypeStruct(right_side.shape, bf16),
        in_specs=[anywhere, anywhere, anywhere, anywhere, scalars, scalars, anywhere, scalars, scalars],
        out_specs=anywhere,
        scratch_shapes=[
            pltpu.VMEM((levels, piece, sn), bf16),
            pltpu.VMEM((levels, sn, sn), bf16),
            pltpu.VMEM((levels, sn, sn), bf16),
            pltpu.VMEM((levels - 1, slots, sn, sn), bf16),
            pltpu.VMEM((levels - 1, slots, sn, sn), bf16),
            pltpu.VMEM((levels, piece, sn), bf16),
            pltpu.VMEM((levels, piece, sn), bf16),
            pltpu.VMEM((steps, chains, nrhs // chains, sn), bf16),
            pltpu.VMEM((chains, nrhs // chains, sn), jnp.float32),
            pltpu.VMEM((steps, chains, ncol - 1, piece // chains, sn), bf16),
            pltpu.VMEM((steps, chains, group * nrhs // chains, sn), bf16),
            pltpu.VMEM((chains, levels * group + 1, nrhs // chains, sn), bf16),
            pltpu.VMEM((chains, levels * group + 1, nrhs // chains, sn), bf16),
            dma, dma((levels,)), dma((levels,)), dma((levels - 1,)), dma((levels - 1,)),
            dma((steps,)), dma((steps, chains)), dma((steps,)), dma((steps, chains)), dma((levels,)), dma,
        ],
        compiler_params=pltpu.CompilerParams(
            collective_id=0, has_side_effects=True, vmem_limit_bytes=60 * 1024 * 1024
        ),
        cost_estimate=pl.CostEstimate(flops=1200000000, bytes_accessed=10000000, transcendentals=0),
    )(right_side, lower_inverse, upper_inverse,
      lower_blocks, jnp.swapaxes(lower_sources, 0, 1), jnp.swapaxes(lower_counts, 1, 2),
      upper_blocks, jnp.swapaxes(upper_sources, 0, 1), jnp.swapaxes(upper_counts, 1, 2))


def solution(mesh):
    in_specs = (
        P("prow", None, None, None),
        P("prow", None, None, None),
        P("prow", None, None, None),
        P("prow", None, "pcol", None, None),
        P("prow", None, "pcol"),
        P("prow", None, "pcol"),
        P("prow", None, "pcol", None, None),
        P("prow", None, "pcol"),
        P("prow", None, "pcol"),
    )
    out_specs = P("prow", None, None, None)
    return jax.shard_map(shards, mesh=mesh, in_specs=in_specs, out_specs=out_specs, check_vma=False)
```

time: 103 us -> 92.4 us (0.90)
  local copies, waits for them, and re-layouts: 6.96 us -> 1.77 us
  Pallas kernels: 95.4 us -> 90.4 us
    unnamed x5 -> x1, local copies, waits for them, and re-layouts: 6.96 us -> 1.77 us
    pallas_call x1, Pallas kernels: 95.4 us -> 90.4 us  [shards(): pl.pallas_call(functools.partial(kernel, width, ncol, chains), out_shape=...]
where the time goes in v2:
time: 92.4 us; the launch traced here: 92.2 us
  Pallas kernels  90.4 us (98%)
  local copies, waits for them, and re-layouts  1.77 us (2%)
    pallas_call x1, Pallas kernels, shards(): pl.pallas_call(functools.partial(kernel, width, ncol, chains), out_shape=...  90.4 us

profile of v2, /device:TPU:0, one launch (start us, length us, event | category | flops | bytes accessed | tf_op | source)
XLA Modules:
  0.0 92.2 jit_solution(16369653810948322831)
XLA Ops:
  0.0 90.4 %shard_map.91 = bf16[1,6,128,256]{3,2,1,0:T(8,128)(2,1)} custom-call(bf16[1,6,128,256]{3,2,1,0:T(8,128)(2,1)} %right_hbm.1, bf16[1,6,256,256]{3,2,1,0:T(8,128)(2,1)} %linv_hbm.1, bf16[1,6,256,256]{3,2,1,0:T(8,128)(2,1)} %uinv_hbm.1, bf16[1,5,6,256,256]{4,3,2,1,0:T(8,128)(2,1)} %lblk_hbm.1, s32[5,1,6]{2,1,0:T(1,128)} %bitcast.4, s32[1,1,5]{2,1,0:T(1,128)} %bitcast.6, ...), custom_call_target="tpu_custom_call" | custom-call | flops 1200000000 | bytes 10000000 | tf_op jit(solution)/shard_map/pallas_call | solution.py:230
  90.4 1.8 %copy.11 = bf16[1,6,128,256]{3,2,1,0:T(8,128)(2,1)} copy(bf16[1,6,128,256]{3,2,1,0:T(8,128)(2,1)} %shard_map.91) | data formatting | bytes 786432

commit v3 on v2

--- a/solution.py
+++ b/solution.py
@@ -16,12 +16,12 @@
 
 
 def kernel(
-    width, ncol, chains,
+    width, ncol, inner, chains,
     right_hbm, linv_hbm, uinv_hbm, lblk_hbm, lsrc, lcnt, ublk_hbm, usrc, ucnt,
     out_hbm,
-    right, linv, uinv, lblk, ublk, fown, bown, part, term, red, land, fstore, bstore,
+    right, linv, uinv, lblk, ublk, fown, bown, part, term, red, hop, land, fstore, bstore,
     right_sem, linv_sem, uinv_sem, lblk_sem, ublk_sem,
-    part_send, part_recv, cast_send, cast_recv, out_send, out_recv,
+    part_send, part_recv, cast_send, hop_recv, cast_recv, out_send, out_recv,
 ):
     levels, piece, sn = right.shape
     slots = lblk.shape[1]
@@ -32,7 +32,9 @@
     last = levels - 1
     p = lax.axis_index("prow")
     q = lax.axis_index("pcol")
-    column = lax.rem(p, ncol)
+    outer = width // inner
+    p_out = lax.div(p, inner)
+    p_in = lax.rem(p, inner)
     mine = pl.ds(pl.multiple_of(q * piece, piece), piece)
 
     def load_lower(l):
@@ -59,43 +61,68 @@
         load_uinv(l).start()
 
     barrier = pltpu.get_barrier_semaphore()
-    for o in range(1, ncol):
-        pl.semaphore_signal(barrier, inc=1, device_id=(p, lax.rem(q + o, ncol)), device_id_type=MESH)
-    for g in range(group):
-        row = q + g * ncol
-
-        @pl.when(row != p)
-        def _():
-            for c in range(ncol):
-                pl.semaphore_signal(barrier, inc=1, device_id=(row, c), device_id_type=MESH)
+
+    def greet(row, c):
+        pl.semaphore_signal(barrier, inc=1, device_id=(row, c), device_id_type=MESH)
+
+    for o in range(1, outer):
+        greet(lax.rem(p_out + o, outer) * inner + p_in, q)
+    for i in range(inner):
+        for o in range(0 if i else 1, ncol):
+            greet(p_out * inner + lax.rem(p_in + i, inner), lax.rem(q + o, ncol))
 
     for k in range(chains):
         fstore[k, levels * group] = jnp.zeros((span, sn), jnp.bfloat16)
         bstore[k, levels * group] = jnp.zeros((span, sn), jnp.bfloat16)
-    pl.semaphore_wait(barrier, width + ncol - 2)
-
-    slot_rows = pl.ds(pl.multiple_of(p // ncol * span + q * rows, rows), rows)
-
-    def cast_copy(own, l, step, k, row):
-        return pltpu.make_async_remote_copy(
-            src_ref=own.at[l, pl.ds(k * rows, rows)], dst_ref=land.at[step, k, slot_rows],
-            send_sem=cast_send.at[step], recv_sem=cast_recv.at[step, k],
-            device_id=(row, column), device_id_type=MESH,
-        )
-
-    def cast(own, l, step, k):
-        for j in range(1, width):
-            cast_copy(own, l, step, k, lax.rem(p + j, width)).start()
+    pl.semaphore_wait(barrier, outer + inner * ncol - 2)
+
+    low = p_out < outer // 2
+    edge = jnp.where(low, p_out, outer - 1 - p_out)
+
+    def layer(i):
+        at = jnp.where(i >= edge, i + 1, i)
+        return jnp.where(low, at, outer - 1 - at)
+
+    def forward_piece(piece_ref, step, k, z):
+        origin = z * inner + p_in
+        column = lax.rem(origin, ncol)
+        start = lax.div(origin, ncol) * span + q * rows
+        place = land.at[step, k, pl.ds(pl.multiple_of(start, rows), rows)]
+
+        def send(row):
+            pltpu.make_async_remote_copy(
+                src_ref=piece_ref, dst_ref=place,
+                send_sem=cast_send.at[step], recv_sem=cast_recv.at[step, k],
+                device_id=(row, column), device_id_type=MESH,
+            ).start()
+
+        for i in range(1, inner):
+            send(p_out * inner + lax.rem(p_in + i, inner))
 
         @pl.when(q != column)
         def _():
-            cast_copy(own, l, step, k, p).start()
+            send(p)
 
         @pl.when(q == column)
         def _():
-            pltpu.make_async_copy(
-                own.at[l, pl.ds(k * rows, rows)], land.at[step, k, slot_rows], cast_recv.at[step, k]
+            pltpu.make_async_copy(piece_ref, place, cast_recv.at[step, k]).start()
+
+    def cast(own, l, step, k):
+        piece_ref = own.at[l, pl.ds(k * rows, rows)]
+        for i in range(outer - 2, -1, -1):
+            pltpu.make_async_remote_copy(
+                src_ref=piece_ref, dst_ref=hop.at[step, k, p_out],
+                send_sem=cast_send.at[step], recv_sem=hop_recv.at[step, k, p_out],
+                device_id=(layer(i) * inner + p_in, q), device_id_type=MESH,
             ).start()
+        forward_piece(piece_ref, step, k, p_out)
+
+    def relay(step, k):
+        for i in range(outer - 1):
+            z = layer(i)
+            arrived = hop.at[step, k, z]
+            pltpu.make_async_copy(arrived, arrived, hop_recv.at[step, k, z]).wait()
+            forward_piece(arrived, step, k, z)
 
     def receive(store, l, step, k):
         whole = land.at[step, k]
@@ -153,6 +180,8 @@
         load_lower(l - 1).wait()
         load_linv(l).wait()
         for k in range(chains):
+            relay(l - 1, k)
+        for k in range(chains):
             receive(fstore, l - 1, l - 1, k)
             contract(l - 1, l - 1, k, lblk, lsrc, lcnt, fstore)
         for k in range(chains):
@@ -178,6 +207,8 @@
         load_upper(l).wait()
         load_uinv(l).wait()
         for k in range(chains):
+            relay(step, k)
+        for k in range(chains):
             receive(bstore, l + 1, step, k)
             contract(step, l, k, ublk, usrc, ucnt, bstore)
         for k in range(chains):
@@ -199,10 +230,12 @@
             sent = land.at[step, k, pl.ds(0, (width - 1) * rows)]
             pltpu.make_async_copy(sent, sent, cast_send.at[step]).wait()
 
-        @pl.when(q != column)
-        def _():
-            one = land.at[step, 0, pl.ds(0, piece)]
-            pltpu.make_async_copy(one, one, cast_send.at[step]).wait()
+        for z in range(outer):
+
+            @pl.when(q != lax.rem(z * inner + p_in, ncol))
+            def _():
+                one = land.at[step, 0, pl.ds(0, piece)]
+                pltpu.make_async_copy(one, one, cast_send.at[step]).wait()
 
         return 0
 
@@ -222,13 +255,16 @@
     slots = lower_blocks.shape[2]
     piece = nrhs // ncol
     chains = 2 if piece % 32 == 0 else 1
+    inner = 1
+    while inner * inner * 4 <= width:
+        inner *= 2
     steps = 2 * (levels - 1)
     bf16 = jnp.bfloat16
     anywhere = pl.BlockSpec(memory_space=pl.ANY)
     scalars = pl.BlockSpec(memory_space=pltpu.SMEM)
     dma = pltpu.SemaphoreType.DMA
     return pl.pallas_call(
-        functools.partial(kernel, width, ncol, chains),
+        functools.partial(kernel, width, ncol, inner, chains),
         out_shape=jax.ShapeDtypeStruct(right_side.shape, bf16),
         in_specs=[anywhere, anywhere, anywhere, anywhere, scalars, scalars, anywhere, scalars, scalars],
         out_specs=anywhere,
@@ -243,11 +279,12 @@
             pltpu.VMEM((steps, chains, nrhs // chains, sn), bf16),
             pltpu.VMEM((chains, nrhs // chains, sn), jnp.float32),
             pltpu.VMEM((steps, chains, ncol - 1, piece // chains, sn), bf16),
+            pltpu.VMEM((steps, chains, width // inner, piece // chains, sn), bf16),
             pltpu.VMEM((steps, chains, group * nrhs // chains, sn), bf16),
             pltpu.VMEM((chains, levels * group + 1, nrhs // chains, sn), bf16),
             pltpu.VMEM((chains, levels * group + 1, nrhs // chains, sn), bf16),
             dma, dma((levels,)), dma((levels,)), dma((levels - 1,)), dma((levels - 1,)),
-            dma((steps,)), dma((steps, chains)), dma((steps,)), dma((steps, chains)), dma((levels,)), dma,
+            dma((steps,)), dma((steps, chains)), dma((steps,)), dma((steps, chains, width // inner)), dma((steps, chains)), dma((levels,)), dma,
         ],
         compiler_params=pltpu.CompilerParams(
             collective_id=0, has_side_effects=True, vmem_limit_bytes=60 * 1024 * 1024

time: 92.4 us -> 110 us (1.19)
  Pallas kernels: 90.4 us -> 108 us
    pallas_call x1, Pallas kernels: 90.4 us -> 108 us  [shards(): pl.pallas_call(functools.partial(kernel, width, ncol, inner, chains), out...]
where the time goes in v3:
time: 110 us; the launch traced here: 109 us
  Pallas kernels  108 us (98%)
  local copies, waits for them, and re-layouts  1.77 us (2%)
    pallas_call x1, Pallas kernels, shards(): pl.pallas_call(functools.partial(kernel, width, ncol, inner, chains), out...  108 us

profile of v3, /device:TPU:0, one launch (start us, length us, event | category | flops | bytes accessed | tf_op | source)
XLA Modules:
  0.0 109.4 jit_solution(4503850389700277099)
XLA Ops:
  0.0 107.6 %shard_map.91 = bf16[1,6,128,256]{3,2,1,0:T(8,128)(2,1)} custom-call(bf16[1,6,128,256]{3,2,1,0:T(8,128)(2,1)} %right_hbm.1, bf16[1,6,256,256]{3,2,1,0:T(8,128)(2,1)} %linv_hbm.1, bf16[1,6,256,256]{3,2,1,0:T(8,128)(2,1)} %uinv_hbm.1, bf16[1,5,6,256,256]{4,3,2,1,0:T(8,128)(2,1)} %lblk_hbm.1, s32[5,1,6]{2,1,0:T(1,128)} %bitcast.4, s32[1,1,5]{2,1,0:T(1,128)} %bitcast.6, ...), custom_call_target="tpu_custom_call" | custom-call | flops 1200000000 | bytes 10000000 | tf_op jit(solution)/shard_map/pallas_call | solution.py:266
  107.6 1.8 %copy.11 = bf16[1,6,128,256]{3,2,1,0:T(8,128)(2,1)} copy(bf16[1,6,128,256]{3,2,1,0:T(8,128)(2,1)} %shard_map.91) | data formatting | bytes 786432

commit v4 on v2

--- a/solution.py
+++ b/solution.py
@@ -19,7 +19,7 @@
     width, ncol, chains,
     right_hbm, linv_hbm, uinv_hbm, lblk_hbm, lsrc, lcnt, ublk_hbm, usrc, ucnt,
     out_hbm,
-    right, linv, uinv, lblk, ublk, fown, bown, part, term, red, land, fstore, bstore,
+    right, linv, uinv, lblk, ublk, fown, bown, part, term, red, land, fstore, bstore, sums, past,
     right_sem, linv_sem, uinv_sem, lblk_sem, ublk_sem,
     part_send, part_recv, cast_send, cast_recv, out_send, out_recv,
 ):
@@ -69,9 +69,9 @@
             for c in range(ncol):
                 pl.semaphore_signal(barrier, inc=1, device_id=(row, c), device_id_type=MESH)
 
-    for k in range(chains):
-        fstore[k, levels * group] = jnp.zeros((span, sn), jnp.bfloat16)
-        bstore[k, levels * group] = jnp.zeros((span, sn), jnp.bfloat16)
+    fstore[levels * group] = jnp.zeros((nrhs, sn), jnp.bfloat16)
+    bstore[levels * group] = jnp.zeros((nrhs, sn), jnp.bfloat16)
+    past[...] = jnp.zeros_like(past)
     pl.semaphore_wait(barrier, width + ncol - 2)
 
     slot_rows = pl.ds(pl.multiple_of(p // ncol * span + q * rows, rows), rows)
@@ -97,21 +97,48 @@
                 own.at[l, pl.ds(k * rows, rows)], land.at[step, k, slot_rows], cast_recv.at[step, k]
             ).start()
 
-    def receive(store, l, step, k):
-        whole = land.at[step, k]
-        pltpu.make_async_copy(whole, whole, cast_recv.at[step, k]).wait()
-        for g in range(group):
-            store[k, l * group + g] = land[step, k, pl.ds(g * span, span)]
-
-    def contract(step, at, k, blocks, sources, counts, store):
+    def keep(store, l, step):
+        for k in range(chains):
+            for g in range(group):
+                store[l * group + g, pl.ds(k * span, span)] = land[step, k, pl.ds(g * span, span)]
+
+    def gather_newest(at, newest, blocks, sources, counts):
+        count = counts[0, 0, at]
+        weights = []
+        for c in range(slots):
+            source = sources[at, 0, c]
+            fits = jnp.logical_and(c < count, lax.div(source, width) == newest)
+            place = jnp.where(fits, lax.div(lax.rem(source, width), ncol), group)
+            weights.append([jnp.where(place == g, 1.0, 0.0).astype(jnp.float32) for g in range(group)])
+        height = sn // 4
+        for r in range(0, sn, height):
+            total = [None] * group
+            for c in range(slots):
+                block = blocks[at, c, pl.ds(r, height)].astype(jnp.float32)
+                for g in range(group):
+                    now = block * weights[c][g]
+                    total[g] = now if total[g] is None else total[g] + now
+            for g in range(group):
+                sums[g, pl.ds(r, height)] = total[g].astype(jnp.bfloat16)
+
+    def add_older(at, newest, blocks, sources, counts, store):
         count = counts[0, 0, at]
         total = None
         for c in range(slots):
             source = sources[at, 0, c]
-            place = lax.div(source, width) * group + lax.div(lax.rem(source, width), ncol)
-            place = jnp.where(c < count, place, levels * group)
-            now = product(store[k, place], blocks[at, c])
+            level = lax.div(source, width)
+            place = level * group + lax.div(lax.rem(source, width), ncol)
+            fits = jnp.logical_and(c < count, level != newest)
+            now = product(store[jnp.where(fits, place, levels * group)], blocks[at, c])
             total = now if total is None else total + now
+        past[...] = total
+
+    def contract(step, k):
+        whole = land.at[step, k]
+        pltpu.make_async_copy(whole, whole, cast_recv.at[step, k]).wait()
+        total = past[pl.ds(k * span, span)]
+        for g in range(group):
+            total = total + product(land[step, k, pl.ds(g * span, span)], sums[g])
         part[step, k] = total.astype(jnp.bfloat16)
         for o in range(1, ncol):
             peer = lax.rem(q + o, ncol)
@@ -148,19 +175,30 @@
     fown[0] = product(right[0], linv[0]).astype(jnp.bfloat16)
     for k in range(chains):
         cast(fown, 0, 0, k)
+    load_lower(0).wait()
+    gather_newest(0, 0, lblk, lsrc, lcnt)
 
     def forward(l, _):
-        load_lower(l - 1).wait()
+        for k in range(chains):
+            contract(l - 1, k)
+
+        @pl.when(l < last)
+        def _():
+            load_lower(l).wait()
+            gather_newest(l, l, lblk, lsrc, lcnt)
+            keep(fstore, l - 1, l - 1)
+
         load_linv(l).wait()
-        for k in range(chains):
-            receive(fstore, l - 1, l - 1, k)
-            contract(l - 1, l - 1, k, lblk, lsrc, lcnt, fstore)
         for k in range(chains):
             finish(l - 1, l, k, right, linv, fown)
 
             @pl.when(l < last)
             def _():
                 cast(fown, l, l, k)
+
+        @pl.when(l < last)
+        def _():
+            add_older(l, l, lblk, lsrc, lcnt, fstore)
 
         return 0
 
@@ -171,15 +209,23 @@
     for k in range(chains):
         cast(bown, last, last, k)
     hand_out(last)
+    load_upper(last - 1).wait()
+    gather_newest(last - 1, last, ublk, usrc, ucnt)
+    past[...] = jnp.zeros_like(past)
 
     def backward(i, _):
         l = last - 1 - i
         step = last + i
-        load_upper(l).wait()
+        for k in range(chains):
+            contract(step, k)
+
+        @pl.when(l > 0)
+        def _():
+            load_upper(l - 1).wait()
+            gather_newest(l - 1, l, ublk, usrc, ucnt)
+            keep(bstore, l + 1, step)
+
         load_uinv(l).wait()
-        for k in range(chains):
-            receive(bstore, l + 1, step, k)
-            contract(step, l, k, ublk, usrc, ucnt, bstore)
         for k in range(chains):
             finish(step, l, k, fown, uinv, bown)
 
@@ -188,6 +234,11 @@
                 cast(bown, l, step + 1, k)
 
         hand_out(l)
+
+        @pl.when(l > 0)
+        def _():
+            add_older(l - 1, l, ublk, usrc, ucnt, bstore)
+
         return 0
 
     lax.fori_loop(0, last, backward, 0)
@@ -244,8 +295,10 @@
             pltpu.VMEM((chains, nrhs // chains, sn), jnp.float32),
             pltpu.VMEM((steps, chains, ncol - 1, piece // chains, sn), bf16),
             pltpu.VMEM((steps, chains, group * nrhs // chains, sn), bf16),
-            pltpu.VMEM((chains, levels * group + 1, nrhs // chains, sn), bf16),
-            pltpu.VMEM((chains, levels * group + 1, nrhs // chains, sn), bf16),
+            pltpu.VMEM((levels * group + 1, nrhs, sn), bf16),
+            pltpu.VMEM((levels * group + 1, nrhs, sn), bf16),
+            pltpu.VMEM((group, sn, sn), bf16),
+            pltpu.VMEM((nrhs, sn), jnp.float32),
             dma, dma((levels,)), dma((levels,)), dma((levels - 1,)), dma((levels - 1,)),
             dma((steps,)), dma((steps, chains)), dma((steps,)), dma((steps, chains)), dma((levels,)), dma,
         ],

time: 92.4 us -> 88.9 us (0.962)
  Pallas kernels: 90.4 us -> 87 us
    pallas_call x1, Pallas kernels: 90.4 us -> 87 us  [shards(): pl.pallas_call(functools.partial(kernel, width, ncol, chains), out_shape=...]
where the time goes in v4:
time: 88.9 us; the launch traced here: 88.7 us
  Pallas kernels  87 us (98%)
  local copies, waits for them, and re-layouts  1.77 us (2%)
    pallas_call x1, Pallas kernels, shards(): pl.pallas_call(functools.partial(kernel, width, ncol, chains), out_shape=...  87 us

profile of v4, /device:TPU:0, one launch (start us, length us, event | category | flops | bytes accessed | tf_op | source)
XLA Modules:
  0.0 88.7 jit_solution(5384495705676256966)
XLA Ops:
  0.0 87.0 %shard_map.91 = bf16[1,6,128,256]{3,2,1,0:T(8,128)(2,1)} custom-call(bf16[1,6,128,256]{3,2,1,0:T(8,128)(2,1)} %right_hbm.1, bf16[1,6,256,256]{3,2,1,0:T(8,128)(2,1)} %linv_hbm.1, bf16[1,6,256,256]{3,2,1,0:T(8,128)(2,1)} %uinv_hbm.1, bf16[1,5,6,256,256]{4,3,2,1,0:T(8,128)(2,1)} %lblk_hbm.1, s32[5,1,6]{2,1,0:T(1,128)} %bitcast.4, s32[1,1,5]{2,1,0:T(1,128)} %bitcast.6, ...), custom_call_target="tpu_custom_call" | custom-call | flops 1200000000 | bytes 10000000 | tf_op jit(solution)/shard_map/pallas_call | solution.py:281
  87.0 1.8 %copy.11 = bf16[1,6,128,256]{3,2,1,0:T(8,128)(2,1)} copy(bf16[1,6,128,256]{3,2,1,0:T(8,128)(2,1)} %shard_map.91) | data formatting | bytes 786432

commit v5 on v4

--- a/solution.py
+++ b/solution.py
@@ -69,8 +69,9 @@
             for c in range(ncol):
                 pl.semaphore_signal(barrier, inc=1, device_id=(row, c), device_id_type=MESH)
 
-    fstore[levels * group] = jnp.zeros((nrhs, sn), jnp.bfloat16)
-    bstore[levels * group] = jnp.zeros((nrhs, sn), jnp.bfloat16)
+    for k in range(chains):
+        fstore[k, levels * group] = jnp.zeros((span, sn), jnp.bfloat16)
+        bstore[k, levels * group] = jnp.zeros((span, sn), jnp.bfloat16)
     past[...] = jnp.zeros_like(past)
     pl.semaphore_wait(barrier, width + ncol - 2)
 
@@ -97,10 +98,9 @@
                 own.at[l, pl.ds(k * rows, rows)], land.at[step, k, slot_rows], cast_recv.at[step, k]
             ).start()
 
-    def keep(store, l, step):
-        for k in range(chains):
-            for g in range(group):
-                store[l * group + g, pl.ds(k * span, span)] = land[step, k, pl.ds(g * span, span)]
+    def keep(store, l, step, k):
+        for g in range(group):
+            store[k, l * group + g] = land[step, k, pl.ds(g * span, span)]
 
     def gather_newest(at, newest, blocks, sources, counts):
         count = counts[0, 0, at]
@@ -121,7 +121,7 @@
             for g in range(group):
                 sums[g, pl.ds(r, height)] = total[g].astype(jnp.bfloat16)
 
-    def add_older(at, newest, blocks, sources, counts, store):
+    def add_older(at, newest, k, blocks, sources, counts, store):
         count = counts[0, 0, at]
         total = None
         for c in range(slots):
@@ -129,14 +129,14 @@
             level = lax.div(source, width)
             place = level * group + lax.div(lax.rem(source, width), ncol)
             fits = jnp.logical_and(c < count, level != newest)
-            now = product(store[jnp.where(fits, place, levels * group)], blocks[at, c])
+            now = product(store[k, jnp.where(fits, place, levels * group)], blocks[at, c])
             total = now if total is None else total + now
-        past[...] = total
+        past[k] = total
 
     def contract(step, k):
         whole = land.at[step, k]
         pltpu.make_async_copy(whole, whole, cast_recv.at[step, k]).wait()
-        total = past[pl.ds(k * span, span)]
+        total = past[k]
         for g in range(group):
             total = total + product(land[step, k, pl.ds(g * span, span)], sums[g])
         part[step, k] = total.astype(jnp.bfloat16)
@@ -179,17 +179,20 @@
     gather_newest(0, 0, lblk, lsrc, lcnt)
 
     def forward(l, _):
+        load_linv(l).wait()
+
+        @pl.when(l < last)
+        def _():
+            load_lower(l).wait()
+
         for k in range(chains):
             contract(l - 1, k)
 
-        @pl.when(l < last)
-        def _():
-            load_lower(l).wait()
-            gather_newest(l, l, lblk, lsrc, lcnt)
-            keep(fstore, l - 1, l - 1)
-
-        load_linv(l).wait()
-        for k in range(chains):
+            @pl.when(l < last)
+            def _():
+                keep(fstore, l - 1, l - 1, k)
+                add_older(l, l, k, lblk, lsrc, lcnt, fstore)
+
             finish(l - 1, l, k, right, linv, fown)
 
             @pl.when(l < last)
@@ -198,7 +201,7 @@
 
         @pl.when(l < last)
         def _():
-            add_older(l, l, lblk, lsrc, lcnt, fstore)
+            gather_newest(l, l, lblk, lsrc, lcnt)
 
         return 0
 
@@ -216,17 +219,20 @@
     def backward(i, _):
         l = last - 1 - i
         step = last + i
+        load_uinv(l).wait()
+
+        @pl.when(l > 0)
+        def _():
+            load_upper(l - 1).wait()
+
         for k in range(chains):
             contract(step, k)
 
-        @pl.when(l > 0)
-        def _():
-            load_upper(l - 1).wait()
-            gather_newest(l - 1, l, ublk, usrc, ucnt)
-            keep(bstore, l + 1, step)
-
-        load_uinv(l).wait()
-        for k in range(chains):
+            @pl.when(l > 0)
+            def _():
+                keep(bstore, l + 1, step, k)
+                add_older(l - 1, l, k, ublk, usrc, ucnt, bstore)
+
             finish(step, l, k, fown, uinv, bown)
 
             @pl.when(l > 0)
@@ -237,7 +243,7 @@
 
         @pl.when(l > 0)
         def _():
-            add_older(l - 1, l, ublk, usrc, ucnt, bstore)
+            gather_newest(l - 1, l, ublk, usrc, ucnt)
 
         return 0
 
@@ -295,10 +301,10 @@
             pltpu.VMEM((chains, nrhs // chains, sn), jnp.float32),
             pltpu.VMEM((steps, chains, ncol - 1, piece // chains, sn), bf16),
             pltpu.VMEM((steps, chains, group * nrhs // chains, sn), bf16),
-            pltpu.VMEM((levels * group + 1, nrhs, sn), bf16),
-            pltpu.VMEM((levels * group + 1, nrhs, sn), bf16),
+            pltpu.VMEM((chains, levels * group + 1, nrhs // chains, sn), bf16),
+            pltpu.VMEM((chains, levels * group + 1, nrhs // chains, sn), bf16),
             pltpu.VMEM((group, sn, sn), bf16),
-            pltpu.VMEM((nrhs, sn), jnp.float32),
+            pltpu.VMEM((chains, nrhs // chains, sn), jnp.float32),
             dma, dma((levels,)), dma((levels,)), dma((levels - 1,)), dma((levels - 1,)),
             dma((steps,)), dma((steps, chains)), dma((steps,)), dma((steps, chains)), dma((levels,)), dma,
         ],

time: 88.9 us -> 92.8 us (1.044)
  Pallas kernels: 87 us -> 90.8 us
    pallas_call x1, Pallas kernels: 87 us -> 90.8 us  [shards(): pl.pallas_call(functools.partial(kernel, width, ncol, chains), out_shape=...]
where the time goes in v5:
time: 92.8 us; the launch traced here: 92.6 us
  Pallas kernels  90.8 us (98%)
  local copies, waits for them, and re-layouts  1.77 us (2%)
    pallas_call x1, Pallas kernels, shards(): pl.pallas_call(functools.partial(kernel, width, ncol, chains), out_shape=...  90.8 us

profile of v5, /device:TPU:0, one launch (start us, length us, event | category | flops | bytes accessed | tf_op | source)
XLA Modules:
  0.0 92.6 jit_solution(13667236216087368461)
XLA Ops:
  0.0 90.8 %shard_map.91 = bf16[1,6,128,256]{3,2,1,0:T(8,128)(2,1)} custom-call(bf16[1,6,128,256]{3,2,1,0:T(8,128)(2,1)} %right_hbm.1, bf16[1,6,256,256]{3,2,1,0:T(8,128)(2,1)} %linv_hbm.1, bf16[1,6,256,256]{3,2,1,0:T(8,128)(2,1)} %uinv_hbm.1, bf16[1,5,6,256,256]{4,3,2,1,0:T(8,128)(2,1)} %lblk_hbm.1, s32[5,1,6]{2,1,0:T(1,128)} %bitcast.4, s32[1,1,5]{2,1,0:T(1,128)} %bitcast.6, ...), custom_call_target="tpu_custom_call" | custom-call | flops 1200000000 | bytes 10000000 | tf_op jit(solution)/shard_map/pallas_call | solution.py:287
  90.8 1.8 %copy.11 = bf16[1,6,128,256]{3,2,1,0:T(8,128)(2,1)} copy(bf16[1,6,128,256]{3,2,1,0:T(8,128)(2,1)} %shard_map.91) | data formatting | bytes 786432

commit v6 on v5

--- a/solution.py
+++ b/solution.py
@@ -23,17 +23,15 @@
     right_sem, linv_sem, uinv_sem, lblk_sem, ublk_sem,
     part_send, part_recv, cast_send, cast_recv, out_send, out_recv,
 ):
-    levels, piece, sn = right.shape
+    levels, nrhs, sn = right.shape
     slots = lblk.shape[1]
     group = width // ncol
-    nrhs = piece * ncol
-    rows = piece // chains
     span = nrhs // chains
     last = levels - 1
     p = lax.axis_index("prow")
     q = lax.axis_index("pcol")
     column = lax.rem(p, ncol)
-    mine = pl.ds(pl.multiple_of(q * piece, piece), piece)
+    owner = q == column
 
     def load_lower(l):
         return pltpu.make_async_copy(lblk_hbm.at[0, l], lblk.at[l], lblk_sem.at[l])
@@ -47,7 +45,7 @@
     def load_uinv(l):
         return pltpu.make_async_copy(uinv_hbm.at[0, l], uinv.at[l], uinv_sem.at[l])
 
-    load_right = pltpu.make_async_copy(right_hbm.at[0, :, mine], right, right_sem)
+    load_right = pltpu.make_async_copy(right_hbm.at[0], right, right_sem)
     load_linv(0).start()
     load_right.start()
     for l in range(last):
@@ -59,44 +57,52 @@
         load_uinv(l).start()
 
     barrier = pltpu.get_barrier_semaphore()
-    for o in range(1, ncol):
-        pl.semaphore_signal(barrier, inc=1, device_id=(p, lax.rem(q + o, ncol)), device_id_type=MESH)
+
+    def greet(row, c):
+        pl.semaphore_signal(barrier, inc=1, device_id=(row, c), device_id_type=MESH)
+
     for g in range(group):
         row = q + g * ncol
 
         @pl.when(row != p)
         def _():
-            for c in range(ncol):
-                pl.semaphore_signal(barrier, inc=1, device_id=(row, c), device_id_type=MESH)
+            greet(row, q)
+
+    @pl.when(owner)
+    def _():
+        for o in range(1, ncol):
+            greet(p, lax.rem(q + o, ncol))
+
+    @pl.when(jnp.logical_not(owner))
+    def _():
+        greet(p, column)
 
     for k in range(chains):
         fstore[k, levels * group] = jnp.zeros((span, sn), jnp.bfloat16)
         bstore[k, levels * group] = jnp.zeros((span, sn), jnp.bfloat16)
     past[...] = jnp.zeros_like(past)
-    pl.semaphore_wait(barrier, width + ncol - 2)
-
-    slot_rows = pl.ds(pl.multiple_of(p // ncol * span + q * rows, rows), rows)
-
-    def cast_copy(own, l, step, k, row):
-        return pltpu.make_async_remote_copy(
-            src_ref=own.at[l, pl.ds(k * rows, rows)], dst_ref=land.at[step, k, slot_rows],
-            send_sem=cast_send.at[step], recv_sem=cast_recv.at[step, k],
-            device_id=(row, column), device_id_type=MESH,
-        )
+
+    @pl.when(owner)
+    def _():
+        pl.semaphore_wait(barrier, width + ncol - 2)
+
+    @pl.when(jnp.logical_not(owner))
+    def _():
+        pl.semaphore_wait(barrier, 1)
+
+
+    slot_rows = pl.ds(pl.multiple_of(lax.div(p, ncol) * span, span), span)
 
     def cast(own, l, step, k):
+        piece = own.at[l, pl.ds(k * span, span)]
+        place = land.at[step, k, slot_rows]
         for j in range(1, width):
-            cast_copy(own, l, step, k, lax.rem(p + j, width)).start()
-
-        @pl.when(q != column)
-        def _():
-            cast_copy(own, l, step, k, p).start()
-
-        @pl.when(q == column)
-        def _():
-            pltpu.make_async_copy(
-                own.at[l, pl.ds(k * rows, rows)], land.at[step, k, slot_rows], cast_recv.at[step, k]
+            pltpu.make_async_remote_copy(
+                src_ref=piece, dst_ref=place,
+                send_sem=cast_send.at[step], recv_sem=cast_recv.at[step, k],
+                device_id=(lax.rem(p + j, width), column), device_id_type=MESH,
             ).start()
+        pltpu.make_async_copy(piece, place, cast_recv.at[step, k]).start()
 
     def keep(store, l, step, k):
         for g in range(group):
@@ -139,42 +145,49 @@
         total = past[k]
         for g in range(group):
             total = total + product(land[step, k, pl.ds(g * span, span)], sums[g])
-        part[step, k] = total.astype(jnp.bfloat16)
-        for o in range(1, ncol):
-            peer = lax.rem(q + o, ncol)
+
+        @pl.when(owner)
+        def _():
+            term[k] = total
+
+        @pl.when(jnp.logical_not(owner))
+        def _():
+            part[step, k] = total.astype(jnp.bfloat16)
             pltpu.make_async_remote_copy(
-                src_ref=part.at[step, k, pl.ds(pl.multiple_of(peer * rows, rows), rows)],
-                dst_ref=red.at[step, k, o - 1],
+                src_ref=part.at[step, k], dst_ref=red.at[step, k, lax.rem(q - column + ncol, ncol) - 1],
                 send_sem=part_send.at[step], recv_sem=part_recv.at[step, k],
-                device_id=(p, peer), device_id_type=MESH,
+                device_id=(p, column), device_id_type=MESH,
             ).start()
-        term[k] = total
 
     def finish(step, row, k, right_ref, inverse, own):
-        update = term[k, pl.ds(pl.multiple_of(q * rows, rows), rows)]
         arrived = red.at[step, k]
         pltpu.make_async_copy(arrived, arrived, part_recv.at[step, k]).wait()
+        update = term[k]
         for o in range(ncol - 1):
             update = update + red[step, k, o].astype(jnp.float32)
-        here = pl.ds(k * rows, rows)
+        here = pl.ds(k * span, span)
         residual = (right_ref[row, here].astype(jnp.float32) - update).astype(jnp.bfloat16)
         own[row, here] = product(residual, inverse[row]).astype(jnp.bfloat16)
 
     def hand_out(l):
-        place = out_hbm.at[0, l, mine]
         for o in range(1, ncol):
             pltpu.make_async_remote_copy(
-                src_ref=bown.at[l], dst_ref=place,
-                send_sem=out_send.at[l], recv_sem=out_recv,
+                src_ref=bown.at[l], dst_ref=out_hbm.at[0, l],
+                send_sem=out_send, recv_sem=out_recv,
                 device_id=(p, lax.rem(q + o, ncol)), device_id_type=MESH,
             ).start()
-        pltpu.make_async_copy(bown.at[l], place, out_recv).start()
+        pltpu.make_async_copy(bown.at[l], out_hbm.at[0, l], out_recv).start()
 
     load_linv(0).wait()
     load_right.wait()
-    fown[0] = product(right[0], linv[0]).astype(jnp.bfloat16)
-    for k in range(chains):
-        cast(fown, 0, 0, k)
+
+    @pl.when(owner)
+    def _():
+        for k in range(chains):
+            here = pl.ds(k * span, span)
+            fown[0, here] = product(right[0, here], linv[0]).astype(jnp.bfloat16)
+            cast(fown, 0, 0, k)
+
     load_lower(0).wait()
     gather_newest(0, 0, lblk, lsrc, lcnt)
 
@@ -193,11 +206,13 @@
                 keep(fstore, l - 1, l - 1, k)
                 add_older(l, l, k, lblk, lsrc, lcnt, fstore)
 
-            finish(l - 1, l, k, right, linv, fown)
-
-            @pl.when(l < last)
+            @pl.when(owner)
             def _():
-                cast(fown, l, l, k)
+                finish(l - 1, l, k, right, linv, fown)
+
+                @pl.when(l < last)
+                def _():
+                    cast(fown, l, l, k)
 
         @pl.when(l < last)
         def _():
@@ -208,10 +223,15 @@
     lax.fori_loop(1, levels, forward, 0)
 
     load_uinv(last).wait()
-    bown[last] = product(fown[last], uinv[last]).astype(jnp.bfloat16)
-    for k in range(chains):
-        cast(bown, last, last, k)
-    hand_out(last)
+
+    @pl.when(owner)
+    def _():
+        for k in range(chains):
+            here = pl.ds(k * span, span)
+            bown[last, here] = product(fown[last, here], uinv[last]).astype(jnp.bfloat16)
+            cast(bown, last, last, k)
+        hand_out(last)
+
     load_upper(last - 1).wait()
     gather_newest(last - 1, last, ublk, usrc, ucnt)
     past[...] = jnp.zeros_like(past)
@@ -233,13 +253,17 @@
                 keep(bstore, l + 1, step, k)
                 add_older(l - 1, l, k, ublk, usrc, ucnt, bstore)
 
-            finish(step, l, k, fown, uinv, bown)
-
-            @pl.when(l > 0)
+            @pl.when(owner)
             def _():
-                cast(bown, l, step + 1, k)
-
-        hand_out(l)
+                finish(step, l, k, fown, uinv, bown)
+
+                @pl.when(l > 0)
+                def _():
+                    cast(bown, l, step + 1, k)
+
+        @pl.when(owner)
+        def _():
+            hand_out(l)
 
         @pl.when(l > 0)
         def _():
@@ -249,24 +273,27 @@
 
     lax.fori_loop(0, last, backward, 0)
 
-    def drain(step, _):
-        sent = red.at[step]
-        pltpu.make_async_copy(sent, sent, part_send.at[step]).wait()
-        for k in range(chains):
-            sent = land.at[step, k, pl.ds(0, (width - 1) * rows)]
-            pltpu.make_async_copy(sent, sent, cast_send.at[step]).wait()
-
-        @pl.when(q != column)
-        def _():
-            one = land.at[step, 0, pl.ds(0, piece)]
-            pltpu.make_async_copy(one, one, cast_send.at[step]).wait()
-
-        return 0
-
-    lax.fori_loop(0, 2 * last, drain, 0)
-    for l in range(levels):
-        sent = red.at[0]
-        pltpu.make_async_copy(sent, sent, out_send.at[l]).wait()
+    @pl.when(owner)
+    def _():
+        def drain(step, _):
+            sent = part.at[step]
+            for j in range(1, width):
+                pltpu.make_async_copy(sent, sent, cast_send.at[step]).wait()
+            return 0
+
+        lax.fori_loop(0, 2 * last, drain, 0)
+        for o in range(1, ncol):
+            pltpu.make_async_copy(out_hbm.at[0], out_hbm.at[0], out_send).wait()
+
+    @pl.when(jnp.logical_not(owner))
+    def _():
+        def drain(step, _):
+            sent = part.at[step]
+            pltpu.make_async_copy(sent, sent, part_send.at[step]).wait()
+            return 0
+
+        lax.fori_loop(0, 2 * last, drain, 0)
+
     pltpu.make_async_copy(out_hbm.at[0], out_hbm.at[0], out_recv).wait()
 
 
@@ -277,8 +304,8 @@
     group = width // ncol
     _, levels, nrhs, sn = right_side.shape
     slots = lower_blocks.shape[2]
-    piece = nrhs // ncol
-    chains = 2 if piece % 32 == 0 else 1
+    chains = 2
+    span = nrhs // chains
     steps = 2 * (levels - 1)
     bf16 = jnp.bfloat16
     anywhere = pl.BlockSpec(memory_space=pl.ANY)
@@ -290,23 +317,23 @@
         in_specs=[anywhere, anywhere, anywhere, anywhere, scalars, scalars, anywhere, scalars, scalars],
         out_specs=anywhere,
         scratch_shapes=[
-            pltpu.VMEM((levels, piece, sn), bf16),
+            pltpu.VMEM((levels, nrhs, sn), bf16),
             pltpu.VMEM((levels, sn, sn), bf16),
             pltpu.VMEM((levels, sn, sn), bf16),
             pltpu.VMEM((levels - 1, slots, sn, sn), bf16),
             pltpu.VMEM((levels - 1, slots, sn, sn), bf16),
-            pltpu.VMEM((levels, piece, sn), bf16),
-            pltpu.VMEM((levels, piece, sn), bf16),
-            pltpu.VMEM((steps, chains, nrhs // chains, sn), bf16),
-            pltpu.VMEM((chains, nrhs // chains, sn), jnp.float32),
-            pltpu.VMEM((steps, chains, ncol - 1, piece // chains, sn), bf16),
-            pltpu.VMEM((steps, chains, group * nrhs // chains, sn), bf16),
-            pltpu.VMEM((chains, levels * group + 1, nrhs // chains, sn), bf16),
-            pltpu.VMEM((chains, levels * group + 1, nrhs // chains, sn), bf16),
+            pltpu.VMEM((levels, nrhs, sn), bf16),
+            pltpu.VMEM((levels, nrhs, sn), bf16),
+            pltpu.VMEM((steps, chains, span, sn), bf16),
+            pltpu.VMEM((chains, span, sn), jnp.float32),
+            pltpu.VMEM((steps, chains, ncol - 1, span, sn), bf16),
+            pltpu.VMEM((steps, chains, group * span, sn), bf16),
+            pltpu.VMEM((chains, levels * group + 1, span, sn), bf16),
+            pltpu.VMEM((chains, levels * group + 1, span, sn), bf16),
             pltpu.VMEM((group, sn, sn), bf16),
-            pltpu.VMEM((chains, nrhs // chains, sn), jnp.float32),
+            pltpu.VMEM((chains, span, sn), jnp.float32),
             dma, dma((levels,)), dma((levels,)), dma((levels - 1,)), dma((levels - 1,)),
-            dma((steps,)), dma((steps, chains)), dma((steps,)), dma((steps, chains)), dma((levels,)), dma,
+            dma((steps,)), dma((steps, chains)), dma((steps,)), dma((steps, chains)), dma, dma,
         ],
         compiler_params=pltpu.CompilerParams(
             collective_id=0, has_side_effects=True, vmem_limit_bytes=60 * 1024 * 1024

time: 92.8 us -> 95.6 us (1.030)
  Pallas kernels: 90.8 us -> 93.6 us
    pallas_call x1, Pallas kernels: 90.8 us -> 93.6 us  [shards(): pl.pallas_call(functools.partial(kernel, width, ncol, chains), out_shape=...]
where the time goes in v6:
time: 95.6 us; the launch traced here: 95.4 us
  Pallas kernels  93.6 us (98%)
  local copies, waits for them, and re-layouts  1.77 us (2%)
    pallas_call x1, Pallas kernels, shards(): pl.pallas_call(functools.partial(kernel, width, ncol, chains), out_shape=...  93.6 us

profile of v6, /device:TPU:0, one launch (start us, length us, event | category | flops | bytes accessed | tf_op | source)
XLA Modules:
  0.0 95.4 jit_solution(17214734460592231975)
XLA Ops:
  0.0 93.6 %shard_map.91 = bf16[1,6,128,256]{3,2,1,0:T(8,128)(2,1)} custom-call(bf16[1,6,128,256]{3,2,1,0:T(8,128)(2,1)} %right_hbm.1, bf16[1,6,256,256]{3,2,1,0:T(8,128)(2,1)} %linv_hbm.1, bf16[1,6,256,256]{3,2,1,0:T(8,128)(2,1)} %uinv_hbm.1, bf16[1,5,6,256,256]{4,3,2,1,0:T(8,128)(2,1)} %lblk_hbm.1, s32[5,1,6]{2,1,0:T(1,128)} %bitcast.4, s32[1,1,5]{2,1,0:T(1,128)} %bitcast.6, ...), custom_call_target="tpu_custom_call" | custom-call | flops 1200000000 | bytes 10000000 | tf_op jit(solution)/shard_map/pallas_call | solution.py:314
  93.6 1.8 %copy.11 = bf16[1,6,128,256]{3,2,1,0:T(8,128)(2,1)} copy(bf16[1,6,128,256]{3,2,1,0:T(8,128)(2,1)} %shard_map.91) | data formatting | bytes 786432

commit v7 on v5

--- a/solution.py
+++ b/solution.py
@@ -69,9 +69,8 @@
             for c in range(ncol):
                 pl.semaphore_signal(barrier, inc=1, device_id=(row, c), device_id_type=MESH)
 
-    for k in range(chains):
-        fstore[k, levels * group] = jnp.zeros((span, sn), jnp.bfloat16)
-        bstore[k, levels * group] = jnp.zeros((span, sn), jnp.bfloat16)
+    fstore[levels * group] = jnp.zeros((nrhs, sn), jnp.bfloat16)
+    bstore[levels * group] = jnp.zeros((nrhs, sn), jnp.bfloat16)
     past[...] = jnp.zeros_like(past)
     pl.semaphore_wait(barrier, width + ncol - 2)
 
@@ -100,9 +99,9 @@
 
     def keep(store, l, step, k):
         for g in range(group):
-            store[k, l * group + g] = land[step, k, pl.ds(g * span, span)]
-
-    def gather_newest(at, newest, blocks, sources, counts):
+            store[l * group + g, pl.ds(k * span, span)] = land[step, k, pl.ds(g * span, span)]
+
+    def gather_newest(step, at, newest, blocks, sources, counts):
         count = counts[0, 0, at]
         weights = []
         for c in range(slots):
@@ -119,9 +118,9 @@
                     now = block * weights[c][g]
                     total[g] = now if total[g] is None else total[g] + now
             for g in range(group):
-                sums[g, pl.ds(r, height)] = total[g].astype(jnp.bfloat16)
-
-    def add_older(at, newest, k, blocks, sources, counts, store):
+                sums[lax.rem(step, 2), g, pl.ds(r, height)] = total[g].astype(jnp.bfloat16)
+
+    def add_older(at, newest, blocks, sources, counts, store):
         count = counts[0, 0, at]
         total = None
         for c in range(slots):
@@ -129,16 +128,16 @@
             level = lax.div(source, width)
             place = level * group + lax.div(lax.rem(source, width), ncol)
             fits = jnp.logical_and(c < count, level != newest)
-            now = product(store[k, jnp.where(fits, place, levels * group)], blocks[at, c])
+            now = product(store[jnp.where(fits, place, levels * group)], blocks[at, c])
             total = now if total is None else total + now
-        past[k] = total
+        past[...] = total
 
     def contract(step, k):
         whole = land.at[step, k]
         pltpu.make_async_copy(whole, whole, cast_recv.at[step, k]).wait()
-        total = past[k]
+        total = past[pl.ds(k * span, span)]
         for g in range(group):
-            total = total + product(land[step, k, pl.ds(g * span, span)], sums[g])
+            total = total + product(land[step, k, pl.ds(g * span, span)], sums[lax.rem(step, 2), g])
         part[step, k] = total.astype(jnp.bfloat16)
         for o in range(1, ncol):
             peer = lax.rem(q + o, ncol)
@@ -176,7 +175,7 @@
     for k in range(chains):
         cast(fown, 0, 0, k)
     load_lower(0).wait()
-    gather_newest(0, 0, lblk, lsrc, lcnt)
+    gather_newest(jnp.int32(0), 0, 0, lblk, lsrc, lcnt)
 
     def forward(l, _):
         load_linv(l).wait()
@@ -191,17 +190,16 @@
             @pl.when(l < last)
             def _():
                 keep(fstore, l - 1, l - 1, k)
-                add_older(l, l, k, lblk, lsrc, lcnt, fstore)
+                if k == 0:
+                    gather_newest(l, l, l, lblk, lsrc, lcnt)
+                if k == chains - 1:
+                    add_older(l, l, lblk, lsrc, lcnt, fstore)
 
             finish(l - 1, l, k, right, linv, fown)
 
             @pl.when(l < last)
             def _():
                 cast(fown, l, l, k)
-
-        @pl.when(l < last)
-        def _():
-            gather_newest(l, l, lblk, lsrc, lcnt)
 
         return 0
 
@@ -213,7 +211,7 @@
         cast(bown, last, last, k)
     hand_out(last)
     load_upper(last - 1).wait()
-    gather_newest(last - 1, last, ublk, usrc, ucnt)
+    gather_newest(jnp.int32(last), last - 1, last, ublk, usrc, ucnt)
     past[...] = jnp.zeros_like(past)
 
     def backward(i, _):
@@ -231,7 +229,10 @@
             @pl.when(l > 0)
             def _():
                 keep(bstore, l + 1, step, k)
-                add_older(l - 1, l, k, ublk, usrc, ucnt, bstore)
+                if k == 0:
+                    gather_newest(step + 1, l - 1, l, ublk, usrc, ucnt)
+                if k == chains - 1:
+                    add_older(l - 1, l, ublk, usrc, ucnt, bstore)
 
             finish(step, l, k, fown, uinv, bown)
 
@@ -240,10 +241,6 @@
                 cast(bown, l, step + 1, k)
 
         hand_out(l)
-
-        @pl.when(l > 0)
-        def _():
-            gather_newest(l - 1, l, ublk, usrc, ucnt)
 
         return 0
 
@@ -301,10 +298,10 @@
             pltpu.VMEM((chains, nrhs // chains, sn), jnp.float32),
             pltpu.VMEM((steps, chains, ncol - 1, piece // chains, sn), bf16),
             pltpu.VMEM((steps, chains, group * nrhs // chains, sn), bf16),
-            pltpu.VMEM((chains, levels * group + 1, nrhs // chains, sn), bf16),
-            pltpu.VMEM((chains, levels * group + 1, nrhs // chains, sn), bf16),
-            pltpu.VMEM((group, sn, sn), bf16),
-            pltpu.VMEM((chains, nrhs // chains, sn), jnp.float32),
+            pltpu.VMEM((levels * group + 1, nrhs, sn), bf16),
+            pltpu.VMEM((levels * group + 1, nrhs, sn), bf16),
+            pltpu.VMEM((2, group, sn, sn), bf16),
+            pltpu.VMEM((nrhs, sn), jnp.float32),
             dma, dma((levels,)), dma((levels,)), dma((levels - 1,)), dma((levels - 1,)),
             dma((steps,)), dma((steps, chains)), dma((steps,)), dma((steps, chains)), dma((levels,)), dma,
         ],

time: 92.8 us -> 92.9 us (level)
  no operation moved by 1% of the time
where the time goes in v7:
time: 92.9 us; the launch traced here: 92.8 us
  Pallas kernels  91 us (98%)
  local copies, waits for them, and re-layouts  1.77 us (2%)
    pallas_call x1, Pallas kernels, shards(): pl.pallas_call(functools.partial(kernel, width, ncol, chains), out_shape=...  91 us

profile of v7, /device:TPU:0, one launch (start us, length us, event | category | flops | bytes accessed | tf_op | source)
XLA Modules:
  0.0 92.8 jit_solution(17097544758335308546)
XLA Ops:
  0.0 91.0 %shard_map.91 = bf16[1,6,128,256]{3,2,1,0:T(8,128)(2,1)} custom-call(bf16[1,6,128,256]{3,2,1,0:T(8,128)(2,1)} %right_hbm.1, bf16[1,6,256,256]{3,2,1,0:T(8,128)(2,1)} %linv_hbm.1, bf16[1,6,256,256]{3,2,1,0:T(8,128)(2,1)} %uinv_hbm.1, bf16[1,5,6,256,256]{4,3,2,1,0:T(8,128)(2,1)} %lblk_hbm.1, s32[5,1,6]{2,1,0:T(1,128)} %bitcast.4, s32[1,1,5]{2,1,0:T(1,128)} %bitcast.6, ...), custom_call_target="tpu_custom_call" | custom-call | flops 1200000000 | bytes 10000000 | tf_op jit(solution)/shard_map/pallas_call | solution.py:284
  91.0 1.8 %copy.11 = bf16[1,6,128,256]{3,2,1,0:T(8,128)(2,1)} copy(bf16[1,6,128,256]{3,2,1,0:T(8,128)(2,1)} %shard_map.91) | data formatting | bytes 786432

commit v8 on v4

--- a/solution.py
+++ b/solution.py
@@ -16,7 +16,7 @@
 
 
 def kernel(
-    width, ncol, chains,
+    width, ncol, inner, chains,
     right_hbm, linv_hbm, uinv_hbm, lblk_hbm, lsrc, lcnt, ublk_hbm, usrc, ucnt,
     out_hbm,
     right, linv, uinv, lblk, ublk, fown, bown, part, term, red, land, fstore, bstore, sums, past,
@@ -33,6 +33,9 @@
     p = lax.axis_index("prow")
     q = lax.axis_index("pcol")
     column = lax.rem(p, ncol)
+    outer = width // inner
+    p_out = lax.div(p, inner)
+    p_in = lax.rem(p, inner)
     mine = pl.ds(pl.multiple_of(q * piece, piece), piece)
 
     def load_lower(l):
@@ -76,6 +79,13 @@
 
     slot_rows = pl.ds(pl.multiple_of(p // ncol * span + q * rows, rows), rows)
 
+    low = p_out < outer // 2
+    edge = jnp.where(low, p_out, outer - 1 - p_out)
+
+    def layer(i):
+        at = jnp.where(i >= edge, i + 1, i)
+        return jnp.where(low, at, outer - 1 - at)
+
     def cast_copy(own, l, step, k, row):
         return pltpu.make_async_remote_copy(
             src_ref=own.at[l, pl.ds(k * rows, rows)], dst_ref=land.at[step, k, slot_rows],
@@ -84,8 +94,12 @@
         )
 
     def cast(own, l, step, k):
-        for j in range(1, width):
-            cast_copy(own, l, step, k, lax.rem(p + j, width)).start()
+        for i in range(outer - 2, -1, -1):
+            for j in range(inner - 1, -1, -1):
+                row = layer(i) * inner + lax.rem(p_in + j, inner)
+                cast_copy(own, l, step, k, row).start()
+        for j in range(1, inner):
+            cast_copy(own, l, step, k, p_out * inner + lax.rem(p_in + j, inner)).start()
 
         @pl.when(q != column)
         def _():
@@ -140,7 +154,7 @@
         for g in range(group):
             total = total + product(land[step, k, pl.ds(g * span, span)], sums[g])
         part[step, k] = total.astype(jnp.bfloat16)
-        for o in range(1, ncol):
+        for o in sorted(range(1, ncol), key=lambda o: -min(o, ncol - o)):
             peer = lax.rem(q + o, ncol)
             pltpu.make_async_remote_copy(
                 src_ref=part.at[step, k, pl.ds(pl.multiple_of(peer * rows, rows), rows)],
@@ -273,13 +287,16 @@
     slots = lower_blocks.shape[2]
     piece = nrhs // ncol
     chains = 2 if piece % 32 == 0 else 1
+    inner = 1
+    while inner * inner * 4 <= width:
+        inner *= 2
     steps = 2 * (levels - 1)
     bf16 = jnp.bfloat16
     anywhere = pl.BlockSpec(memory_space=pl.ANY)
     scalars = pl.BlockSpec(memory_space=pltpu.SMEM)
     dma = pltpu.SemaphoreType.DMA
     return pl.pallas_call(
-        functools.partial(kernel, width, ncol, chains),
+        functools.partial(kernel, width, ncol, inner, chains),
         out_shape=jax.ShapeDtypeStruct(right_side.shape, bf16),
         in_specs=[anywhere, anywhere, anywhere, anywhere, scalars, scalars, anywhere, scalars, scalars],
         out_specs=anywhere,

time: 88.9 us -> 90 us (1.012)
  Pallas kernels: 87 us -> 88 us
    pallas_call x1, Pallas kernels: 87 us -> 88 us  [shards(): pl.pallas_call(functools.partial(kernel, width, ncol, inner, chains), out...]
where the time goes in v8:
time: 90 us; the launch traced here: 89.8 us
  Pallas kernels  88 us (98%)
  local copies, waits for them, and re-layouts  1.77 us (2%)
    pallas_call x1, Pallas kernels, shards(): pl.pallas_call(functools.partial(kernel, width, ncol, inner, chains), out...  88 us

profile of v8, /device:TPU:0, one launch (start us, length us, event | category | flops | bytes accessed | tf_op | source)
XLA Modules:
  0.0 89.8 jit_solution(5648796302612823579)
XLA Ops:
  0.0 88.0 %shard_map.91 = bf16[1,6,128,256]{3,2,1,0:T(8,128)(2,1)} custom-call(bf16[1,6,128,256]{3,2,1,0:T(8,128)(2,1)} %right_hbm.1, bf16[1,6,256,256]{3,2,1,0:T(8,128)(2,1)} %linv_hbm.1, bf16[1,6,256,256]{3,2,1,0:T(8,128)(2,1)} %uinv_hbm.1, bf16[1,5,6,256,256]{4,3,2,1,0:T(8,128)(2,1)} %lblk_hbm.1, s32[5,1,6]{2,1,0:T(1,128)} %bitcast.4, s32[1,1,5]{2,1,0:T(1,128)} %bitcast.6, ...), custom_call_target="tpu_custom_call" | custom-call | flops 1200000000 | bytes 10000000 | tf_op jit(solution)/shard_map/pallas_call | solution.py:298
  88.0 1.8 %copy.11 = bf16[1,6,128,256]{3,2,1,0:T(8,128)(2,1)} copy(bf16[1,6,128,256]{3,2,1,0:T(8,128)(2,1)} %shard_map.91) | data formatting | bytes 786432
